TPU v7x, 32 devices: a whole 2x2x4 slice. The times are simulated.
32 devices in a mesh: dp: 8 (over z, x), tensor: 4 (over y, core).
Axes of the slice: x: 2, y: 2, z: 4, core: 2. Of those that a mesh axis runs over, the one named last changes fastest.
Arguments:
- tokens: bfloat16 [7680, 4096], P('dp'), may hold values from -70 to 70
- dense_weight: bfloat16 [4096, 14336], P('dp', 'tensor'), may hold values from -0.09375 to 0.09375
- left_factor: bfloat16 [64, 4096], P(None, 'tensor'), may hold values from -0.75 to 0.75
- right_factor: bfloat16 [64, 14336], P(None, 'tensor'), may hold values from -0.75 to 0.75
Outputs:
- dir_left: float32 [64, 4096], P('dp', 'tensor')
- dir_right: float32 [64, 14336], P('dp', 'tensor')
- loss: float32 [], replicated
All inputs are finite; a program needn't handle non-finite values.
Results may differ from a plain program's by a relative error of at most 0.0009.
Values may be sent and summed in bfloat16 or wider, within the bound.
No kernel may reach another device: no remote copies, remote signals or barrier semaphores. Data moves between devices by JAX's collectives and lax.ppermute only.
A program may use at most 128 MiB of HBM per device.

v0:
```python
import jax
import jax.numpy as jnp
from jax import lax
from jax.sharding import PartitionSpec as P

F = 14336
NB = 64
SI = 64
SO = 224
MID = 4096


epsilon = 1e-06


def local(tokens, dense_weight, left_factor, right_factor):
    tok_rows = tokens.shape[0]
    tensor_pos = lax.axis_index("tensor")
    dp_pos = lax.axis_index("dp")
    dp_count = lax.axis_size("dp")
    local_blocks = left_factor.shape[1] // NB
    feature_span = local_blocks * SI
    own_features = lax.dynamic_slice_in_dim(tokens, tensor_pos * feature_span, feature_span, 1)
    own_features = own_features.reshape(tok_rows, local_blocks, SI)
    left_blocks = left_factor.reshape(SI, local_blocks, NB)
    first_mix = jnp.einsum(
        "tik,kij->tji", own_features, left_blocks, preferred_element_type=jnp.float32
    ).astype(jnp.bfloat16)
    permuted = lax.all_to_all(first_mix, "tensor", split_axis=1, concat_axis=2, tiled=True)
    right_blocks = right_factor.reshape(NB, local_blocks, SO)
    output = jnp.einsum("tji,ijo->tjo", permuted, right_blocks, preferred_element_type=jnp.float32)
    output = output.reshape(tok_rows, local_blocks * SO)
    targets = jnp.dot(
        tokens,
        lax.all_gather(dense_weight, "dp", axis=0, tiled=True),
        preferred_element_type=jnp.float32,
    )
    residual = output - targets
    loss_part = jnp.sum(residual * residual)
    total_tokens = tok_rows * dp_count
    slope_rows = (residual / total_tokens).astype(jnp.bfloat16).reshape(tok_rows, local_blocks, SO)
    grad_right = jnp.einsum(
        "tji,tjo->ijo", permuted, slope_rows, preferred_element_type=jnp.float32
    )
    grad_right = grad_right.reshape(NB, local_blocks * SO)
    back_mix = jnp.einsum(
        "tjo,ijo->tji", slope_rows, right_blocks, preferred_element_type=jnp.float32
    ).astype(jnp.bfloat16)
    all_features = tokens.reshape(tok_rows, NB, SI)
    grad_left = jnp.einsum(
        "tik,tji->kij", all_features, back_mix, preferred_element_type=jnp.float32
    )
    left_sum, right_sum, loss_dp = lax.psum((grad_left, grad_right, loss_part), "dp")
    sq_left, sq_right, loss_all = lax.psum(
        (jnp.sum(left_sum * left_sum), jnp.sum(right_sum * right_sum), loss_dp), "tensor"
    )
    rows_left = SI // dp_count
    rows_right = NB // dp_count
    left_rows = lax.dynamic_slice_in_dim(left_sum, dp_pos * rows_left, rows_left, 0)
    right_rows = lax.dynamic_slice_in_dim(right_sum, dp_pos * rows_right, rows_right, 0)
    left_rows = lax.all_to_all(left_rows, "tensor", split_axis=1, concat_axis=2, tiled=True)
    left_rows = left_rows.reshape(left_rows.shape[0], local_blocks * NB)
    dir_left = left_rows * lax.rsqrt(sq_left / (SI * MID) + epsilon)
    dir_right = right_rows * lax.rsqrt(sq_right / (NB * F) + epsilon)
    loss = loss_all / (2.0 * total_tokens)
    return (dir_left, dir_right, loss)


def solution(mesh):
    in_specs = (P("dp", None), P("dp", "tensor"), P(None, "tensor"), P(None, "tensor"))
    out_specs = (P("dp", "tensor"), P("dp", "tensor"), P())
    return jax.shard_map(local, mesh=mesh, in_specs=in_specs, out_specs=out_specs, check_vma=False)
```

profile of v0, /device:TPU:0, one launch (start us, length us, event | category | flops | bytes accessed | tf_op | source)
XLA Modules:
  0.0 754.3 jit_solution(18096828806357781446)
XLA Ops:
  7.2 0.0 copy-start.3
  7.2 0.0 all-gather.2.cloned.1.call-start
  7.2 0.7 all-gather.2.cloned.1.call-update
  7.9 3.0 constant_dynamic-slice_fusion.1
  10.9 2.8 copy.24
  13.8 0.0 copy-done.3
  13.8 0.2 copy.37
  14.0 0.7 convert_bitcast_fusion
  14.7 2.5 copy.26
  17.2 4.2 all-to-all-start
  21.4 0.0 copy-start.2
  21.4 0.0 all-reduce.4.cloned.1.call-start
  21.4 12.0 %copy.32 = bf16[960,4096]{0,1:T(8,128)(2,1)} copy(bf16[960,4096]{1,0:T(8,128)(2,1)} %param.4) | data formatting | bytes 15728640 | tf_op args[0]
  33.4 0.0 copy-done.2
  33.4 0.7 reshape.35
  34.1 13.0 %all-to-all-done = bf16[960,64,16]{0,2,1:T(8,128)(2,1)S(1)} async-done(((bf16[960,64,16]{0,2,1:T(8,128)(2,1)}), bf16[960,64,16]{0,2,1:T(8,128)(2,1)S(1)}, u32[]{:S(2)}, u32[]{:S(2)}) %all-to-all-start) | async-done | bytes 1966112 | tf_op jit(solution)/shard_map/all_to_all | solution.py:29
  47.1 0.0 copy-start.1
  47.1 1.4 copy-done.1
  48.5 1.8 copy.27
  50.3 7.3 fusion.6
  57.6 15.0 %copy.29 = f32[960,3584]{1,0:T(8,128)} copy(f32[960,3584]{0,1:T(8,128)} %bitcast.34) | data formatting | bytes 27525120 | tf_op jit(solution)/shard_map/reshape | solution.py:32
  72.6 498.8 %all-gather.2.cloned.1.call-done = bf16[4096,3584]{1,0:T(8,128)(2,1)} async-done(((bf16[512,3584]{1,0:T(8,128)(2,1)}), bf16[4096,3584]{1,0:T(8,128)(2,1)}) %all-gather.2.cloned.1.call-update) | async-done | bytes 29360144 | tf_op jit(solution)/shard_map/all_gather | solution.py:35
  571.4 37.9 %multiply_reduce_fusion = (f32[]{:T(128)}, bf16[960,3584]{1,0:T(8,128)(2,1)}) fusion(f32[960,3584]{1,0:T(8,128)} %copy.29, bf16[960,4096]{1,0:T(8,128)(2,1)} %param.4, bf16[4096,3584]{1,0:T(8,128)(2,1)} %all-gather.2.cloned.1.call-done), kind=kOutput, calls=%fused_computation | convolution fusion | flops 28202926080 | bytes 57868292 | tf_op jit(solution)/shard_map/dot_general | solution.py:33
  609.3 10.3 %copy.30 = bf16[960,3584]{0,1:T(8,128)(2,1)} copy(bf16[960,3584]{1,0:T(8,128)(2,1)} %get-tuple-element.9) | data formatting | bytes 13762560 | tf_op jit(solution)/shard_map/convert_element_type | solution.py:41
  619.6 0.0 copy-start
  619.6 5.6 convolution_bitcast_fusion
  625.2 0.0 copy-done
  625.2 1.4 convolution_convert_fusion
  626.6 0.6 copy.36
  627.2 1.6 reshape.39
  628.8 6.5 fusion.2
  635.3 0.0 all-reduce.4.cloned.1.call-update
  635.3 21.2 %psum.46 = f32[]{:T(128)} all-reduce(f32[]{:T(128)} %get-tuple-element.8), channel_id=1, replica_groups=mesh['dp'=8,'tensor'=4] {'dp'}, use_global_device_ids=true, to_apply=%region_7.0 | all-reduce | flops 1 | bytes 8 | tf_op jit(solution)/shard_map/psum | solution.py:53
  656.6 65.9 %all-reduce.4.cloned.1.call-done = (f32[64,64,16]{0,2,1:T(8,128)}, f32[64,3584]{1,0:T(8,128)}) async-done(((f32[64,64,16]{0,2,1:T(8,128)}, f32[64,3584]{1,0:T(8,128)}), (f32[64,64,16]{0,2,1:T(8,128)}, f32[64,3584]{1,0:T(8,128)})) %all-reduce.4.cloned.1.call-update) | async-done | bytes 1179664 | tf_op jit(solution)/shard_map/psum | solution.py:53
  722.5 2.0 multiply_reduce_fusion.1
  724.5 1.8 multiply_reduce_fusion.2
  726.3 7.5 all-reduce.1
  734.4 1.2 constant_dynamic-slice_fusion
  735.7 0.2 copy.34
  735.9 0.8 reshape.40
  736.7 3.3 all-to-all-start.1
  739.9 1.6 dynamic-slice_multiply_fusion
  742.8 1.1 all-to-all-done.1
  743.9 0.5 broadcast.7
  744.4 0.7 reduce
  745.1 0.1 reshape.41
  745.3 0.2 copy.35
  745.4 0.9 mul.44
  (1 shorter events, 0.0 us)
Async XLA Ops:
  7.2 6.6 copy-start.3
  7.2 564.2 %all-gather.2.cloned.1.call-start = ((), (), s32[]{:S(2)}) async-start(), calls=%async_computation.2 | async-start | bytes 33030144 | tf_op jit(solution)/shard_map/all_gather | solution.py:35
  17.2 30.0 %all-to-all-start = ((bf16[960,64,16]{0,2,1:T(8,128)(2,1)}), bf16[960,64,16]{0,2,1:T(8,128)(2,1)S(1)}, u32[]{:S(2)}, u32[]{:S(2)}) async-start(bf16[960,64,16]{0,2,1:T(8,128)(2,1)} %copy.26), calls=%async_computation | async-start | bytes 4194304 | tf_op jit(solution)/shard_map/all_to_all | solution.py:29
  21.4 12.0 %copy-start.2 = (bf16[64,3584]{1,0:T(8,128)(2,1)S(1)}, bf16[64,3584]{1,0:T(8,128)(2,1)}, u32[]{:S(2)}) copy-start(bf16[64,3584]{1,0:T(8,128)(2,1)} %param.7) | copy-start | bytes 1376260
  21.4 701.1 %all-reduce.4.cloned.1.call-start = ((), (), s32[]{:S(2)}) async-start(), calls=%async_computation.3 | async-start | bytes 2883584 | tf_op jit(solution)/shard_map/psum | solution.py:53
  47.1 1.4 copy-start.1
  619.6 5.6 copy-start
  736.7 7.2 all-to-all-start.1
Sparse Core Ops, SparseCore 0:
  9.5 561.7 all-gather.1
  635.5 86.9 all-reduce.3
where the time goes:
time: 756 us; the launch traced here: 754 us
  waiting for transfers between devices  579 us (77%)
  matrix products  59.4 us (8%)
  local copies, waits for them, and re-layouts  55.8 us (7%)
  blocking collectives  28.7 us (4%)
  between operations  17.3 us (2%)
    all_gather x1, waiting for transfers between devices, local(): lax.all_gather(dense_weight, 'dp', axis=0, tiled=True)  499 us
    psum x1, waiting for transfers between devices, local(): lax.psum((grad_left, grad_right, loss_part), 'dp')  65.9 us
    dot_general x1, matrix products, local(): jnp.dot(tokens, lax.all_gather(dense_weight, 'dp', axis=0, tiled=True), p...  37.9 us
    psum x1, blocking collectives, local(): lax.psum((grad_left, grad_right, loss_part), 'dp')  21.2 us
  transfers between devices with their start and end apart: 4, of which 4 were waited for; matrix products, arithmetic and copies ran while one was open for 6% of the time, Pallas kernels for 0%

commit v1 on v0

v1 whole, which is shorter than its diff:
```python
import jax
import jax.numpy as jnp
from jax import lax
from jax.sharding import PartitionSpec as P

epsilon = 1e-06


def swap(value, axis, stride):
    size = lax.axis_size(axis)
    return lax.ppermute(value, axis, [(a, a ^ stride) for a in range(size)])


def ordered(value, axis, strides):
    position = lax.axis_index(axis)
    for stride in strides:
        other = swap(value, axis, stride)
        high = (position // stride) % 2 == 1
        value = jnp.concatenate([jnp.where(high, other, value), jnp.where(high, value, other)], 0)
    return value


def local(tokens, dense_weight, left_factor, right_factor):
    tok_rows, features = tokens.shape
    weight_rows, columns = dense_weight.shape
    dp_count = lax.axis_size("dp")
    tensor_count = lax.axis_size("tensor")
    dp_pos = lax.axis_index("dp")
    tensor_pos = lax.axis_index("tensor")
    in_size = left_factor.shape[0]
    mids = right_factor.shape[0]
    blocks = left_factor.shape[1] * tensor_count // mids
    own_blocks = blocks // tensor_count
    out_size = columns // own_blocks
    total_tokens = tok_rows * dp_count

    bits = dp_count.bit_length() - 1
    strides = [1 << b for b in range(bits)]
    grouped = max(bits - 3, 0)
    pair = strides[grouped:][len(strides[grouped:]) // 2]
    others = [s for s in reversed(strides[grouped:]) if s != pair]
    pair_bit = (dp_pos // pair) % 2
    unit_rows = weight_rows << grouped

    half_blocks = own_blocks // 2
    chunks = 2 if half_blocks % 2 == 0 else 1
    chunk_blocks = half_blocks // chunks
    chunk_columns = chunk_blocks * out_size
    half_columns = half_blocks * out_size

    def weight_piece(half, chunk):
        start = half * half_columns + chunk * chunk_columns
        return lax.dynamic_slice_in_dim(dense_weight, start, chunk_columns, 1)

    gathered = []
    for chunk in range(chunks):
        mine = ordered(weight_piece(pair_bit, chunk), "dp", strides[:grouped])
        theirs = ordered(weight_piece(1 - pair_bit, chunk), "dp", strides[:grouped])
        held = {0: mine, pair: swap(theirs, "dp", pair)}
        for stride in others:
            for mask in list(held):
                held[mask ^ stride] = swap(held[mask], "dp", stride)
        gathered.append(held)

    share = tok_rows // tensor_count
    part = lax.dynamic_slice_in_dim(tokens, tensor_pos * share, share, 0)
    part = swap(part, "dp", pair)
    partner = ordered(part, "tensor", [1 << b for b in range(tensor_count.bit_length() - 1)])

    left_blocks = left_factor.reshape(in_size, mids // tensor_count, blocks)
    left_blocks = lax.all_to_all(left_blocks, "tensor", split_axis=2, concat_axis=1, tiled=True)
    left_blocks = lax.dynamic_slice_in_dim(left_blocks, pair_bit * half_blocks, half_blocks, 2)
    eye_left = jnp.eye(mids, dtype=jnp.bfloat16)
    left_rows = left_blocks.transpose(1, 0, 2)
    left_diag = (left_rows[:, :, :, None] * eye_left[:, None, None, :]).reshape(features, half_blocks * mids)
    right_half = lax.dynamic_slice_in_dim(right_factor, pair_bit * half_columns, half_columns, 1)

    column_block = jnp.arange(chunk_columns) // out_size
    row_block = jnp.arange(chunk_blocks * mids) // mids
    same_block = row_block[:, None] == column_block[None, :]
    feature_block = jnp.arange(features) // in_size
    same_mid = jnp.arange(mids)[:, None] == feature_block[None, :]

    token_sets = (tokens, partner)
    mixes = [
        jnp.dot(rows, left_diag, preferred_element_type=jnp.float32).astype(jnp.bfloat16) for rows in token_sets
    ]

    loss_part = jnp.zeros((), jnp.float32)
    right_parts, left_parts = [], []
    for chunk in range(chunks):
        right_chunk = right_half[:, chunk * chunk_columns : (chunk + 1) * chunk_columns]
        right_diag = jnp.where(same_block, jnp.tile(right_chunk, (chunk_blocks, 1)), jnp.bfloat16(0))
        grad_right, grad_left = 0.0, 0.0
        for rows, mix in zip(token_sets, mixes):
            mix_chunk = mix[:, chunk * chunk_blocks * mids : (chunk + 1) * chunk_blocks * mids]
            residual = jnp.dot(mix_chunk, right_diag, preferred_element_type=jnp.float32)
            for mask, piece in gathered[chunk].items():
                start = ((dp_pos ^ mask) >> grouped) * unit_rows
                some = lax.dynamic_slice_in_dim(rows, start, unit_rows, 1)
                residual = residual - jnp.dot(some, piece, preferred_element_type=jnp.float32)
            loss_part = loss_part + jnp.sum(residual * residual)
            slope = (residual / total_tokens).astype(jnp.bfloat16)
            grad_right = grad_right + lax.dot_general(
                mix_chunk, slope, (((0,), (0,)), ((), ())), preferred_element_type=jnp.float32
            )
            back_mix = lax.dot_general(
                slope, right_diag, (((1,), (1,)), ((), ())), preferred_element_type=jnp.float32
            ).astype(jnp.bfloat16)
            grad_left = grad_left + lax.dot_general(
                back_mix, rows, (((0,), (0,)), ((), ())), preferred_element_type=jnp.float32
            )
        right_parts.append(
            jnp.concatenate(
                [
                    grad_right[b * mids : (b + 1) * mids, b * out_size : (b + 1) * out_size]
                    for b in range(chunk_blocks)
                ],
                1,
            )
        )
        left_parts.append(
            jnp.sum(jnp.where(same_mid[None], grad_left.reshape(chunk_blocks, mids, features), 0.0), 1)
        )

    left_sum = jnp.concatenate(left_parts, 0).reshape(half_blocks, mids, in_size).transpose(2, 0, 1)
    both = jnp.concatenate([*right_parts, left_sum.reshape(in_size, half_blocks * mids)], 1)
    width = both.shape[1]
    both = both.reshape((2,) * bits + (both.shape[0] // dp_count, width))
    order = [s for s in reversed(strides)]
    for stride in others + strides[:grouped]:
        at = order.index(stride)
        bit = (dp_pos // stride) % 2
        away = lax.dynamic_index_in_dim(both, 1 - bit, at, keepdims=False)
        kept = lax.dynamic_index_in_dim(both, bit, at, keepdims=False)
        both = kept + swap(away, "dp", stride)
        order.remove(stride)
    away = lax.dynamic_index_in_dim(both, 1 - pair_bit, 0, keepdims=False)
    kept = lax.dynamic_index_in_dim(both, pair_bit, 0, keepdims=False)
    other = swap(away, "dp", pair)
    low = jnp.where(pair_bit == 0, kept, other)
    high = jnp.where(pair_bit == 0, other, kept)
    right_rows = jnp.concatenate([low[:, :half_columns], high[:, :half_columns]], 1)
    left_low = low[:, half_columns:].reshape(-1, half_blocks, mids)
    left_high = high[:, half_columns:].reshape(-1, half_blocks, mids)
    left_rows = jnp.concatenate([left_low, left_high], 1)

    sq_left, sq_right, loss_all = lax.psum(
        (jnp.sum(left_rows * left_rows), jnp.sum(right_rows * right_rows), loss_part), ("dp", "tensor")
    )
    left_rows = lax.all_to_all(left_rows, "tensor", split_axis=2, concat_axis=1, tiled=True)
    left_rows = left_rows.transpose(0, 2, 1).reshape(left_rows.shape[0], -1)
    dir_left = left_rows * lax.rsqrt(sq_left / (features * blocks) + epsilon)
    dir_right = right_rows * lax.rsqrt(sq_right / (mids * columns * tensor_count) + epsilon)
    loss = loss_all / (2.0 * total_tokens)
    return (dir_left, dir_right, loss)


def solution(mesh):
    in_specs = (P("dp", None), P("dp", "tensor"), P(None, "tensor"), P(None, "tensor"))
    out_specs = (P("dp", "tensor"), P("dp", "tensor"), P())
    return jax.shard_map(local, mesh=mesh, in_specs=in_specs, out_specs=out_specs, check_vma=False)
```

time: 756 us -> 549 us (0.73)
  waiting for transfers between devices: 579 us -> 207 us
  matrix products: 59.4 us -> 201 us
  starting transfers between devices: 7.54 us -> 29.8 us
  local copies, waits for them, and re-layouts: 55.8 us -> 36.7 us
  other arithmetic: 6.11 us -> 20.8 us
  blocking collectives: 28.7 us -> 39.2 us
  between operations: 17.3 us -> 7.92 us
    all_gather x1 -> x0, waiting for transfers between devices: 499 us -> none  [local(): lax.all_gather(dense_weight, 'dp', axis=0, tiled=True)]
    ppermute x0 -> x20, waiting for transfers between devices: none -> 205 us  [swap(): return lax.ppermute(value, axis, [(a, a ^ stride) for a in range(size)])]
    dot_general x6 -> x46, matrix products: 59.4 us -> 201 us  [the longest x32 134 us: local(): jnp.dot(some, piece, preferred_element_type=jnp.float32)]
    psum x1 -> x0, waiting for transfers between devices: 65.9 us -> none  [local(): lax.psum((grad_left, grad_right, loss_part), 'dp')]
    ppermute x0 -> x20, starting transfers between devices: none -> 22.7 us  [swap(): return lax.ppermute(value, axis, [(a, a ^ stride) for a in range(size)])]
    reshape x4 -> x5, local copies, waits for them, and re-layouts: 17.5 us -> 2.42 us  [the longest x1 1.71 us: local(): jnp.concatenate(left_parts, 0).reshape(half_blocks, mids, in_size)]
    convert_element_type x2 -> x0, local copies, waits for them, and re-layouts: 12.8 us -> none  [the longest x1 10.3 us: local(): (residual / total_tokens).astype(jnp.bfloat16)]
    all_to_all x2, waiting for transfers between devices: 14 us -> 1.98 us  [the longest x1 1.98 us: local(): lax.all_to_all(left_rows, 'tensor', split_axis=2, concat_axis=1, tiled=True)]
  transfers between devices with their start and end apart: 4 -> 22, of which waited for: 4 -> 11; matrix products, arithmetic and copies ran while one was open for 6% -> 25% of each run, Pallas kernels for 0% -> 0%
where the time goes in v1:
time: 549 us; the launch traced here: 543 us
  waiting for transfers between devices  207 us (38%)
  matrix products  201 us (37%)
  blocking collectives  39.2 us (7%)
  local copies, waits for them, and re-layouts  36.7 us (7%)
  starting transfers between devices  29.8 us (5%)
  other arithmetic  20.8 us (4%)
  between operations  7.92 us (1%)
    ppermute x20, waiting for transfers between devices, swap(): return lax.ppermute(value, axis, [(a, a ^ stride) for a in range(size)])  205 us
    dot_general x32, matrix products, local(): jnp.dot(some, piece, preferred_element_type=jnp.float32)  134 us
    dot_general x4, matrix products, local(): lax.dot_general(back_mix, rows, (((0,), (0,)), ((), ())), preferred_eleme...  41.4 us
    psum x1, blocking collectives, local(): lax.psum((jnp.sum(left_rows * left_rows), jnp.sum(right_rows * right_rows...  39.2 us
    ppermute x20, starting transfers between devices, swap(): return lax.ppermute(value, axis, [(a, a ^ stride) for a in range(size)])  22.7 us
    dot_general x2, matrix products, local(): jnp.dot(rows, left_diag, preferred_element_type=jnp.float32)  12.8 us
    mul x1, local copies, waits for them, and re-layouts, local(): left_rows[:, :, :, None] * eye_left[:, None, None, :]  12 us
  transfers between devices with their start and end apart: 22, of which 11 were waited for; matrix products, arithmetic and copies ran while one was open for 25% of the time, Pallas kernels for 0%

profile of v1, /device:TPU:0, one launch (start us, length us, event | category | flops | bytes accessed | tf_op | source)
XLA Modules:
  0.0 543.1 jit_solution(17460740882548084249)
XLA Ops:
  0.7 3.6 constant_dynamic-slice_fusion.1
  4.3 4.0 collective-permute-start.1
  11.9 3.3 all-to-all-start
  15.2 2.0 collective-permute-start
  17.2 4.4 fusion.41
  21.7 4.1 fusion.39
  25.8 3.1 constant_dynamic-slice_fusion.3
  30.9 7.1 %broadcast_multiply_fusion = bf16[64,64,8,64]{3,2,1,0:T(8,128)(2,1)} fusion(bf16[64,64]{1,0:T(8,128)(2,1)S(1)} %fusion.58, bf16[64,64,8]{2,1,0:T(8,128)(2,1)S(1)} %copy.33), kind=kLoop, calls=%fused_computation.21 | loop fusion | flops 2097152 | bytes 4268032 | tf_op jit(solution)/shard_map/mul | solution.py:75
  38.0 12.0 %mul.126 = bf16[4096,512]{1,0:T(8,128)(2,1)} reshape(bf16[64,64,8,64]{3,2,1,0:T(8,128)(2,1)} %broadcast_multiply_fusion) | data formatting | bytes 8388608 | tf_op jit(solution)/shard_map/mul | solution.py:75
  50.0 8.6 %fusion.2 = bf16[960,512]{1,0:T(8,128)(2,1)S(1)} fusion(bf16[960,4096]{1,0:T(8,128)(2,1)} %param.4, bf16[4096,512]{1,0:T(8,128)(2,1)} %mul.126), kind=kOutput, calls=%fused_computation.42 | convolution fusion | flops 4027023360 | bytes 13041664 | tf_op jit(solution)/shard_map/dot_general | solution.py:86
  60.3 4.8 fusion.25
  65.1 3.7 collective-permute-done
  68.8 2.5 collective-permute-start.7
  71.3 4.1 fusion.37
  75.4 4.1 fusion.23
  79.5 47.8 %collective-permute-done.10 = bf16[512,896]{1,0:T(8,128)(2,1)S(1)} collective-permute-done((bf16[512,896]{1,0:T(8,128)(2,1)S(1)}, bf16[512,896]{1,0:T(8,128)(2,1)S(1)}, u32[]{:S(2)}, u32[]{:S(2)}) %collective-permute-start.10) | collective-permute-done | bytes 917536 | tf_op jit(solution)/shard_map/ppermute | solution.py:11
  128.8 2.9 fusion.35
  133.3 4.2 fusion.33
  138.1 4.1 fusion.31
  142.2 8.1 %collective-permute-done.2 = bf16[512,896]{1,0:T(8,128)(2,1)} collective-permute-done((bf16[512,896]{1,0:T(8,128)(2,1)}, bf16[512,896]{1,0:T(8,128)(2,1)}, u32[]{:S(2)}, u32[]{:S(2)}) %collective-permute-start.2) | collective-permute-done | bytes 917536 | tf_op jit(solution)/shard_map/ppermute | solution.py:11
  151.8 4.2 fusion.29
  156.0 34.2 %collective-permute-done.12 = bf16[512,896]{1,0:T(8,128)(2,1)S(1)} collective-permute-done((bf16[512,896]{1,0:T(8,128)(2,1)S(1)}, bf16[512,896]{1,0:T(8,128)(2,1)S(1)}, u32[]{:S(2)}, u32[]{:S(2)}) %collective-permute-start.12) | collective-permute-done | bytes 917536 | tf_op jit(solution)/shard_map/ppermute | solution.py:11
  191.6 2.9 fusion.27
  195.1 2.9 fusion.17
  200.1 2.9 fusion.15
  203.0 3.0 fusion.21
  206.0 7.3 %collective-permute-done.14 = bf16[512,896]{1,0:T(8,128)(2,1)S(1)} collective-permute-done((bf16[512,896]{1,0:T(8,128)(2,1)S(1)}, bf16[512,896]{1,0:T(8,128)(2,1)S(1)}, u32[]{:S(2)}, u32[]{:S(2)}) %collective-permute-start.14) | collective-permute-done | bytes 917536 | tf_op jit(solution)/shard_map/ppermute | solution.py:11
  213.4 3.0 fusion.19
  216.3 35.4 %collective-permute-done.16 = bf16[512,896]{1,0:T(8,128)(2,1)S(1)} collective-permute-done((bf16[512,896]{1,0:T(8,128)(2,1)S(1)}, bf16[512,896]{1,0:T(8,128)(2,1)S(1)}, u32[]{:S(2)}, u32[]{:S(2)}) %collective-permute-start.16) | collective-permute-done | bytes 917536 | tf_op jit(solution)/shard_map/ppermute | solution.py:11
  251.7 11.2 %multiply_reduce_fusion.1 = (f32[]{:T(128)}, f32[960,896]{1,0:T(8,128)S(1)}) fusion(bf16[512,896]{1,0:T(8,128)(2,1)S(1)} %collective-permute-done.16, bf16[960,4096]{1,0:T(8,128)(2,1)S(1)} %bitcast.98, s32[]{:T(128)S(6)} %select_n.222, f32[960,896]{1,0:T(8,128)} %fusion.15, f32[960,896]{1,0:T(8,128)} %fusion.19, f32[960,896]{1,0:T(8,128)} %fusion.23, ...), kind=kOutput, calls=%fused_computation.26 | convolution fusion | flops 889405440 | bytes 32866312 | tf_op jit(solution)/shard_map/dot_general | solution.py:101
  263.0 2.4 broadcast_select_fusion.3
  265.4 2.1 pad_maximum_fusion.1
  271.8 11.2 %multiply_reduce_fusion.3 = (f32[]{:T(128)}, f32[960,896]{1,0:T(8,128)S(1)}) fusion(bf16[512,896]{1,0:T(8,128)(2,1)} %collective-permute-done.6, bf16[960,4096]{1,0:T(8,128)(2,1)S(1)} %bitcast.98, s32[]{:T(128)S(6)} %select_n.222, f32[960,896]{1,0:T(8,128)} %fusion.17, f32[960,896]{1,0:T(8,128)} %fusion.21, f32[960,896]{1,0:T(8,128)} %fusion.25, ...), kind=kOutput, calls=%fused_computation.28 | convolution fusion | flops 889405440 | bytes 32866312 | tf_op jit(solution)/shard_map/dot_general | solution.py:101
  283.1 1.7 copy-done.4
  286.5 9.4 %fusion.12 = f32[256,4096]{1,0:T(8,128)} fusion(bf16[960,4096]{1,0:T(8,128)(2,1)} %param.4, bf16[256,896]{1,0:T(8,128)(2,1)} %copy-done.11, f32[960,896]{1,0:T(8,128)S(1)} %get-tuple-element.35), kind=kOutput, calls=%fused_computation.61 | convolution fusion | flops 2455633920 | bytes 15958016 | tf_op jit(solution)/shard_map/dot_general | solution.py:110
  295.9 10.6 %fusion.11 = f32[256,4096]{1,0:T(8,128)} fusion(bf16[960,4096]{1,0:T(8,128)(2,1)} %param.4, bf16[256,896]{1,0:T(8,128)(2,1)} %copy-done.9, f32[960,896]{1,0:T(8,128)} %copy-done.4), kind=kOutput, calls=%fused_computation.60 | convolution fusion | flops 2455633920 | bytes 15958016 | tf_op jit(solution)/shard_map/dot_general | solution.py:110
  306.5 48.4 %collective-permute-done.9 = bf16[480,4096]{1,0:T(8,128)(2,1)} collective-permute-done((bf16[480,4096]{1,0:T(8,128)(2,1)}, bf16[480,4096]{1,0:T(8,128)(2,1)}, u32[]{:S(2)}, u32[]{:S(2)}) %collective-permute-start.9) | collective-permute-done | bytes 3932192 | tf_op jit(solution)/shard_map/ppermute | solution.py:11
  354.9 3.8 broadcast_select_fusion
  358.8 5.0 fusion.124
  365.1 4.2 fusion.1
  370.7 2.4 fusion.52
  373.1 2.5 fusion.46
  379.3 4.1 fusion.106
  383.4 4.3 fusion.114
  387.6 2.9 fusion.118
  390.5 9.5 %multiply_reduce_fusion = (f32[]{:T(128)}, f32[960,896]{1,0:T(8,128)}) fusion(bf16[512,896]{1,0:T(8,128)(2,1)} %copy-done.22, s32[]{:T(128)S(6)} %select_n.222, bf16[480,4096]{1,0:T(8,128)(2,1)S(1)} %get-tuple-element.9, bf16[480,4096]{1,0:T(8,128)(2,1)S(1)} %get-tuple-element.8, f32[960,896]{1,0:T(8,128)S(1)} %fusion.98, f32[960,896]{1,0:T(8,128)S(1)} %fusion.102, ...), kind=kOutput, calls=%fused_computation.25 | convolution fusion | flops 891371520 | bytes 39747592 | tf_op jit(solution)/shard_map/dot_general | solution.py:101
  400.1 11.1 %convolution_add_fusion = f32[256,4096]{1,0:T(8,128)} fusion(f32[256,4096]{1,0:T(8,128)} %fusion.12, bf16[480,4096]{1,0:T(8,128)(2,1)} %copy-done, bf16[480,4096]{1,0:T(8,128)(2,1)} %copy-done.2, bf16[256,896]{1,0:T(8,128)(2,1)S(1)} %copy-done.12, f32[960,896]{1,0:T(8,128)} %get-tuple-element.37), kind=kOutput, calls=%fused_computation.17 | convolution fusion | flops 2472411136 | bytes 20152320 | tf_op jit(solution)/shard_map/dot_general | solution.py:110
  411.2 2.8 fusion.120
  415.1 2.4 fusion.116
  417.4 4.2 fusion.112
  421.7 4.3 fusion.108
  425.9 2.9 fusion.104
  428.8 3.0 fusion.100
  431.8 9.4 %multiply_reduce_fusion.2 = (f32[]{:T(128)}, f32[960,896]{1,0:T(8,128)S(1)}) fusion(bf16[512,896]{1,0:T(8,128)(2,1)} %collective-permute-done.6, s32[]{:T(128)S(6)} %select_n.222, bf16[480,4096]{1,0:T(8,128)(2,1)S(1)} %copy-done.3, bf16[480,4096]{1,0:T(8,128)(2,1)S(1)} %copy-done.1, f32[960,896]{1,0:T(8,128)} %fusion.100, f32[960,896]{1,0:T(8,128)} %fusion.104, ...), kind=kOutput, calls=%fused_computation.27 | convolution fusion | flops 891371520 | bytes 39747592 | tf_op jit(solution)/shard_map/dot_general | solution.py:101
  441.2 10.3 %select_reduce_fusion.1 = (f32[4,4096]{1,0:T(4,128)S(1)}, f32[4,4096]{1,0:T(4,128)}) fusion(pred[64,4096]{1,0:T(8,128)(4,1)} %iota_compare_fusion, f32[256,4096]{1,0:T(8,128)} %convolution_add_fusion, f32[256,4096]{1,0:T(8,128)} %fusion.11, bf16[480,4096]{1,0:T(8,128)(2,1)} %copy-done, bf16[480,4096]{1,0:T(8,128)(2,1)} %copy-done.2, ...), kind=kOutput, calls=%fused_computation.20 | convolution fusion | flops 2476572672 | bytes 20545536 | tf_op jit(solution)/shard_map/dot_general | solution.py:110
  454.7 1.8 copy.34
  456.5 1.7 concatenate.48
  458.2 3.2 convolution_add_fusion.2
  464.5 14.2 %collective-permute-done.17 = f32[2,2,8,2304]{3,2,1,0:T(8,128)S(1)} collective-permute-done((f32[2,2,8,2304]{3,2,1,0:T(8,128)S(1)}, f32[2,2,8,2304]{3,2,1,0:T(8,128)S(1)}, u32[]{:S(2)}, u32[]{:S(2)}) %collective-permute-start.17) | collective-permute-done | bytes 294944 | tf_op jit(solution)/shard_map/ppermute | solution.py:11
  480.3 4.3 collective-permute-done.18
  487.2 1.8 collective-permute-done.19
  490.7 39.2 %all-reduce = (f32[]{:T(128)}, f32[]{:T(128)}, f32[]{:T(128)}) all-reduce(f32[]{:T(128)} %multiply_reduce_fusion.5, f32[]{:T(128)} %multiply_reduce_fusion.4, f32[]{:T(128)S(6)} %add.213), channel_id=1, replica_groups=mesh['dp'=8,'tensor'=4] {'dp','tensor'}, use_global_device_ids=true, to_apply=%region_3.4 | all-reduce | flops 3 | bytes 24 | tf_op jit(solution)/shard_map/psum | solution.py:148
  531.4 3.8 all-to-all-start.1
  537.1 2.0 all-to-all-done.1
  (166 shorter events, 42.5 us)
Async XLA Ops:
  0.7 9.7 %copy-start.38 = (bf16[64,1024]{1,0:T(8,128)(2,1)S(1)}, bf16[64,1024]{1,0:T(8,128)(2,1)}, u32[]{:S(2)}) copy-start(bf16[64,1024]{1,0:T(8,128)(2,1)} %param.6) | copy-start | bytes 393220
  4.3 17.3 %copy-start.19 = (bf16[512,896]{1,0:T(8,128)(2,1)}, bf16[512,896]{1,0:T(8,128)(2,1)S(1)}, u32[]{:S(2)}) copy-start(bf16[512,896]{1,0:T(8,128)(2,1)S(1)} %get-tuple-element.15) | copy-start | bytes 2752516
  4.3 127.4 %collective-permute-start.1 = (bf16[512,896]{1,0:T(8,128)(2,1)}, bf16[512,896]{1,0:T(8,128)(2,1)}, u32[]{:S(2)}, u32[]{:S(2)}) collective-permute-start(bf16[512,896]{1,0:T(8,128)(2,1)} %get-tuple-element.14), channel_id=1, source_target_pairs={{0,16},{4,20},{8,24},{12,28},{16,0},{20,4},{24,8},{28,12},{1,17},{... | collective-permute-start | bytes 2752520 | tf_op jit(solution)/shard_map/ppermute | solution.py:11
  8.4 51.7 %collective-permute-start.3 = (bf16[512,896]{1,0:T(8,128)(2,1)}, bf16[512,896]{1,0:T(8,128)(2,1)}, u32[]{:S(2)}, u32[]{:S(2)}) collective-permute-start(bf16[512,896]{1,0:T(8,128)(2,1)} %get-tuple-element.14), channel_id=1, source_target_pairs={{0,4},{4,0},{8,12},{12,8},{16,20},{20,16},{24,28},{28,24},{1,5},{5... | collective-permute-start | bytes 2752520 | tf_op jit(solution)/shard_map/ppermute | solution.py:11
  9.9 127.7 %collective-permute-start.11 = (bf16[512,896]{1,0:T(8,128)(2,1)S(1)}, bf16[512,896]{1,0:T(8,128)(2,1)}, u32[]{:S(2)}, u32[]{:S(2)}) collective-permute-start(bf16[512,896]{1,0:T(8,128)(2,1)S(1)} %get-tuple-element.15), channel_id=1, source_target_pairs={{0,16},{4,20},{8,24},{12,28},{16,0},{20,4},{24,8},{28,12},{1,17},{... | collective-permute-start | bytes 2752520 | tf_op jit(solution)/shard_map/ppermute | solution.py:11
  10.2 65.2 %collective-permute-start.13 = (bf16[512,896]{1,0:T(8,128)(2,1)S(1)}, bf16[512,896]{1,0:T(8,128)(2,1)}, u32[]{:S(2)}, u32[]{:S(2)}) collective-permute-start(bf16[512,896]{1,0:T(8,128)(2,1)S(1)} %get-tuple-element.15), channel_id=1, source_target_pairs={{0,4},{4,0},{8,12},{12,8},{16,20},{20,16},{24,28},{28,24},{1,5},{5... | collective-permute-start | bytes 2752520 | tf_op jit(solution)/shard_map/ppermute | solution.py:11
  11.9 18.2 %all-to-all-start = ((bf16[4,2,8192]{2,1,0:T(2,128)(2,1)}), bf16[4,2,8192]{2,1,0:T(2,128)(2,1)S(1)}, u32[]{:S(2)}, u32[]{:S(2)}) async-start(bf16[4,2,8192]{2,1,0:T(2,128)(2,1)} %reshape.129), calls=%async_computation | async-start | bytes 262144 | tf_op jit(solution)/shard_map/all_to_all | solution.py:71
  15.2 53.6 %collective-permute-start = (bf16[512,896]{1,0:T(8,128)(2,1)}, bf16[512,896]{1,0:T(8,128)(2,1)}, u32[]{:S(2)}, u32[]{:S(2)}) collective-permute-start(bf16[512,896]{1,0:T(8,128)(2,1)} %get-tuple-element.13), channel_id=1, source_target_pairs={{0,8},{4,12},{8,0},{12,4},{16,24},{20,28},{24,16},{28,20},{1,9},{5... | collective-permute-start | bytes 2752520 | tf_op jit(solution)/shard_map/ppermute | solution.py:11
  25.8 4.0 copy-start.39
  30.1 28.6 %copy-start.9 = (bf16[256,896]{1,0:T(8,128)(2,1)}, bf16[256,896]{1,0:T(8,128)(2,1)S(1)}, u32[]{:S(2)}) copy-start(bf16[256,896]{1,0:T(8,128)(2,1)S(1)} %get-tuple-element.29) | copy-start | bytes 1376260
  30.1 29.3 %copy-start.11 = (bf16[256,896]{1,0:T(8,128)(2,1)}, bf16[256,896]{1,0:T(8,128)(2,1)S(1)}, u32[]{:S(2)}) copy-start(bf16[256,896]{1,0:T(8,128)(2,1)S(1)} %get-tuple-element.28) | copy-start | bytes 1376260
  58.6 1.4 copy-start.14
  58.6 1.5 copy-start.37
  58.7 12.6 %slice-start = ((s8[7864320]{0:T(1024)(128)(4,1)}), s8[4194304]{0:T(1024)(128)(4,1)S(1)}, s32[]{:S(2)}) async-start(s8[7864320]{0:T(1024)(128)(4,1)} %bitcast.97), calls=%async_computation.2 | async-start | bytes 8388608
  60.2 8.6 %copy-start.23 = (bf16[240,4096]{1,0:T(8,128)(2,1)S(1)}, bf16[240,4096]{1,0:T(8,128)(2,1)}, u32[]{:S(2)}) copy-start(bf16[240,4096]{1,0:T(8,128)(2,1)} %constant_dynamic-slice_fusion.3) | copy-start | bytes 5898244
  60.2 11.1 %slice-start.1 = ((s8[7864320]{0:T(1024)(128)(4,1)}), s8[3670016]{0:T(1024)(128)(4,1)S(1)}, s32[]{:S(2)}) async-start(s8[7864320]{0:T(1024)(128)(4,1)} %bitcast.97), calls=%async_computation.3 | async-start | bytes 7340032
  60.2 67.1 %collective-permute-start.10 = (bf16[512,896]{1,0:T(8,128)(2,1)S(1)}, bf16[512,896]{1,0:T(8,128)(2,1)S(1)}, u32[]{:S(2)}, u32[]{:S(2)}) collective-permute-start(bf16[512,896]{1,0:T(8,128)(2,1)S(1)} %copy-done.37), channel_id=1, source_target_pairs={{0,8},{4,12},{8,0},{12,4},{16,24},{20,28},{24,16},{28,20},{1,9},{5... | collective-permute-start | bytes 2752520 | tf_op jit(solution)/shard_map/ppermute | solution.py:11
  68.8 130.8 %collective-permute-start.7 = (bf16[240,4096]{1,0:T(8,128)(2,1)S(1)}, bf16[240,4096]{1,0:T(8,128)(2,1)S(1)}, u32[]{:S(2)}, u32[]{:S(2)}) collective-permute-start(bf16[240,4096]{1,0:T(8,128)(2,1)S(1)} %copy-done.23), channel_id=1, source_target_pairs={{0,8},{4,12},{8,0},{12,4},{16,24},{20,28},{24,16},{28,20},{1,9},{5... | collective-permute-start | bytes 5898248 | tf_op jit(solution)/shard_map/ppermute | solution.py:11
  75.4 74.9 %collective-permute-start.2 = (bf16[512,896]{1,0:T(8,128)(2,1)}, bf16[512,896]{1,0:T(8,128)(2,1)}, u32[]{:S(2)}, u32[]{:S(2)}) collective-permute-start(bf16[512,896]{1,0:T(8,128)(2,1)} %collective-permute-done), channel_id=1, source_target_pairs={{0,16},{4,20},{8,24},{12,28},{16,0},{20,4},{24,8},{28,12},{1,17},{... | collective-permute-start | bytes 2752520 | tf_op jit(solution)/shard_map/ppermute | solution.py:11
  127.3 62.8 %copy-start.27 = (bf16[512,896]{1,0:T(8,128)(2,1)}, bf16[512,896]{1,0:T(8,128)(2,1)S(1)}, u32[]{:S(2)}) copy-start(bf16[512,896]{1,0:T(8,128)(2,1)S(1)} %collective-permute-done.10) | copy-start | bytes 2752516
  127.3 75.7 %collective-permute-start.4 = (bf16[512,896]{1,0:T(8,128)(2,1)}, bf16[512,896]{1,0:T(8,128)(2,1)S(1)}, u32[]{:S(2)}, u32[]{:S(2)}) collective-permute-start(bf16[512,896]{1,0:T(8,128)(2,1)} %collective-permute-done), channel_id=1, source_target_pairs={{0,4},{4,0},{8,12},{12,8},{16,20},{20,16},{24,28},{28,24},{1,5},{5... | collective-permute-start | bytes 2752520 | tf_op jit(solution)/shard_map/ppermute | solution.py:11
  131.8 58.4 %collective-permute-start.12 = (bf16[512,896]{1,0:T(8,128)(2,1)S(1)}, bf16[512,896]{1,0:T(8,128)(2,1)S(1)}, u32[]{:S(2)}, u32[]{:S(2)}) collective-permute-start(bf16[512,896]{1,0:T(8,128)(2,1)S(1)} %collective-permute-done.10), channel_id=1, source_target_pairs={{0,16},{4,20},{8,24},{12,28},{16,0},{20,4},{24,8},{28,12},{1,17},{... | collective-permute-start | bytes 2752520 | tf_op jit(solution)/shard_map/ppermute | solution.py:11
  137.6 57.0 %collective-permute-start.5 = (bf16[512,896]{1,0:T(8,128)(2,1)}, bf16[512,896]{1,0:T(8,128)(2,1)S(1)}, u32[]{:S(2)}, u32[]{:S(2)}) collective-permute-start(bf16[512,896]{1,0:T(8,128)(2,1)} %collective-permute-done.1), channel_id=1, source_target_pairs={{0,4},{4,0},{8,12},{12,8},{16,20},{20,16},{24,28},{28,24},{1,5},{5... | collective-permute-start | bytes 2752520 | tf_op jit(solution)/shard_map/ppermute | solution.py:11
  150.3 47.7 %collective-permute-start.15 = (bf16[512,896]{1,0:T(8,128)(2,1)}, bf16[512,896]{1,0:T(8,128)(2,1)S(1)}, u32[]{:S(2)}, u32[]{:S(2)}) collective-permute-start(bf16[512,896]{1,0:T(8,128)(2,1)} %collective-permute-done.11), channel_id=1, source_target_pairs={{0,4},{4,0},{8,12},{12,8},{16,20},{20,16},{24,28},{28,24},{1,5},{5... | collective-permute-start | bytes 2752520 | tf_op jit(solution)/shard_map/ppermute | solution.py:11
  190.1 7.9 %copy-start.31 = (bf16[512,896]{1,0:T(8,128)(2,1)}, bf16[512,896]{1,0:T(8,128)(2,1)S(1)}, u32[]{:S(2)}) copy-start(bf16[512,896]{1,0:T(8,128)(2,1)S(1)} %collective-permute-done.12) | copy-start | bytes 2752516
  190.1 23.2 %collective-permute-start.14 = (bf16[512,896]{1,0:T(8,128)(2,1)S(1)}, bf16[512,896]{1,0:T(8,128)(2,1)S(1)}, u32[]{:S(2)}, u32[]{:S(2)}) collective-permute-start(bf16[512,896]{1,0:T(8,128)(2,1)S(1)} %collective-permute-done.10), channel_id=1, source_target_pairs={{0,4},{4,0},{8,12},{12,8},{16,20},{20,16},{24,28},{28,24},{1,5},{5... | collective-permute-start | bytes 2752520 | tf_op jit(solution)/shard_map/ppermute | solution.py:11
  194.6 3.4 copy-start.29
  194.6 77.2 %collective-permute-start.6 = (bf16[512,896]{1,0:T(8,128)(2,1)}, bf16[512,896]{1,0:T(8,128)(2,1)}, u32[]{:S(2)}, u32[]{:S(2)}) collective-permute-start(bf16[512,896]{1,0:T(8,128)(2,1)} %collective-permute-done.2), channel_id=1, source_target_pairs={{0,4},{4,0},{8,12},{12,8},{16,20},{20,16},{24,28},{28,24},{1,5},{5... | collective-permute-start | bytes 2752520 | tf_op jit(solution)/shard_map/ppermute | solution.py:11
  198.0 5.0 copy-start.33
  198.0 53.7 %collective-permute-start.16 = (bf16[512,896]{1,0:T(8,128)(2,1)S(1)}, bf16[512,896]{1,0:T(8,128)(2,1)S(1)}, u32[]{:S(2)}, u32[]{:S(2)}) collective-permute-start(bf16[512,896]{1,0:T(8,128)(2,1)S(1)} %collective-permute-done.12), channel_id=1, source_target_pairs={{0,4},{4,0},{8,12},{12,8},{16,20},{20,16},{24,28},{28,24},{1,5},{5... | collective-permute-start | bytes 2752520 | tf_op jit(solution)/shard_map/ppermute | solution.py:11
  199.6 3.4 copy-start.24
  200.0 63.0 %collective-permute-start.8 = (bf16[240,4096]{1,0:T(8,128)(2,1)S(1)}, bf16[240,4096]{1,0:T(8,128)(2,1)}, u32[]{:S(2)}, u32[]{:S(2)}) collective-permute-start(bf16[240,4096]{1,0:T(8,128)(2,1)S(1)} %collective-permute-done.7), channel_id=1, source_target_pairs={{0,1},{1,0},{2,3},{3,2},{4,5},{5,4},{6,7},{7,6},{8,9},{9,8},{10,11... | collective-permute-start | bytes 5898248 | tf_op jit(solution)/shard_map/ppermute | solution.py:11
  203.0 3.0 copy-start.25
  213.4 3.0 copy-start.35
  251.7 11.2 %copy-start.22 = (bf16[512,896]{1,0:T(8,128)(2,1)}, bf16[512,896]{1,0:T(8,128)(2,1)S(1)}, u32[]{:S(2)}) copy-start(bf16[512,896]{1,0:T(8,128)(2,1)S(1)} %collective-permute-done.16) | copy-start | bytes 2752516
  265.4 2.6 copy-start.6
  265.4 3.2 copy-start.8
  265.4 4.7 copy-start.15
  268.6 86.3 %collective-permute-start.9 = (bf16[480,4096]{1,0:T(8,128)(2,1)}, bf16[480,4096]{1,0:T(8,128)(2,1)}, u32[]{:S(2)}, u32[]{:S(2)}) collective-permute-start(bf16[480,4096]{1,0:T(8,128)(2,1)} %pad_maximum_fusion.1), channel_id=1, source_target_pairs={{0,2},{1,3},{2,0},{3,1},{4,6},{5,7},{6,4},{7,5},{8,10},{9,11},{10,... | collective-permute-start | bytes 11796488 | tf_op jit(solution)/shard_map/ppermute | solution.py:11
  271.8 13.0 %copy-start.16 = (bf16[960,512]{1,0:T(8,128)(2,1)S(1)}, bf16[960,512]{1,0:T(8,128)(2,1)}, u32[]{:S(2)}) copy-start(bf16[960,512]{1,0:T(8,128)(2,1)} %copy-done.14) | copy-start | bytes 2949124
  283.1 1.7 copy-start.4
  295.9 59.1 %copy-start.7 = (bf16[240,4096]{1,0:T(8,128)(2,1)S(1)}, bf16[240,4096]{1,0:T(8,128)(2,1)}, u32[]{:S(2)}) copy-start(bf16[240,4096]{1,0:T(8,128)(2,1)} %copy-done.6) | copy-start | bytes 5898244
  358.8 31.7 %copy-start = (bf16[480,4096]{1,0:T(8,128)(2,1)}, bf16[480,4096]{1,0:T(8,128)(2,1)S(1)}, u32[]{:S(2)}) copy-start(bf16[480,4096]{1,0:T(8,128)(2,1)S(1)} %get-tuple-element.8) | copy-start | bytes 11796484
  358.8 31.7 %copy-start.2 = (bf16[480,4096]{1,0:T(8,128)(2,1)}, bf16[480,4096]{1,0:T(8,128)(2,1)S(1)}, u32[]{:S(2)}) copy-start(bf16[480,4096]{1,0:T(8,128)(2,1)S(1)} %get-tuple-element.9) | copy-start | bytes 11796484
  358.8 6.3 %copy-start.13 = (bf16[4096,512]{1,0:T(8,128)(2,1)S(1)}, bf16[4096,512]{1,0:T(8,128)(2,1)}, u32[]{:S(2)}) copy-start(bf16[4096,512]{1,0:T(8,128)(2,1)} %mul.126) | copy-start | bytes 12582916
  365.1 4.2 copy-start.20
  369.4 3.8 copy-start.17
  369.4 1.4 copy-start.10
  370.7 2.4 copy-start.12
  370.7 5.0 copy-start.36
  375.7 1.2 copy-start.32
  376.9 1.2 copy-start.34
  383.4 4.3 copy-start.28
  411.2 2.8 copy-start.1
  411.2 3.9 copy-start.3
  421.7 4.3 copy-start.26
  425.9 2.9 copy-start.30
  428.8 3.0 copy-start.5
  458.2 4.0 copy-start.18
  458.2 4.0 copy-start.21
  464.4 14.3 %collective-permute-start.17 = (f32[2,2,8,2304]{3,2,1,0:T(8,128)S(1)}, f32[2,2,8,2304]{3,2,1,0:T(8,128)S(1)}, u32[]{:S(2)}, u32[]{:S(2)}) collective-permute-start(f32[2,2,8,2304]{3,2,1,0:T(8,128)S(1)} %dynamic-slice_bitcast_fusion), channel_id=1, source_target_pairs={{0,16},{4,20},{8,24},{12,28},{16,0},{20,4},{24,8},{28,12},{1,17},{... | collective-permute-start | bytes 884744 | tf_op jit(solution)/shard_map/ppermute | solution.py:11
  478.7 5.8 %collective-permute-start.18 = (f32[2,8,2304]{2,1,0:T(8,128)S(1)}, f32[2,8,2304]{2,1,0:T(8,128)S(1)}, u32[]{:S(2)}, u32[]{:S(2)}) collective-permute-start(f32[2,8,2304]{2,1,0:T(8,128)S(1)} %dynamic-slice_bitcast_fusion.1), channel_id=1, source_target_pairs={{0,4},{4,0},{8,12},{12,8},{16,20},{20,16},{24,28},{28,24},{1,5},{5... | collective-permute-start | bytes 442376 | tf_op jit(solution)/shard_map/ppermute | solution.py:11
  484.6 4.4 collective-permute-start.19
  531.4 7.7 %all-to-all-start.1 = ((f32[4,1,2048]{2,1,0:T(1,128)}), f32[4,1,2048]{2,1,0:T(1,128)S(1)}, u32[]{:S(2)}, u32[]{:S(2)}) async-start(f32[4,1,2048]{2,1,0:T(1,128)} %reshape.131), calls=%async_computation.1 | async-start | bytes 65536 | tf_op jit(solution)/shard_map/all_to_all | solution.py:151

commit v2 on v1

v2 whole, which is shorter than its diff:
```python
import functools

import jax
import jax.numpy as jnp
from jax import lax
from jax.experimental import pallas as pl
from jax.experimental.pallas import tpu as pltpu
from jax.sharding import PartitionSpec as P

epsilon = 1e-06
VMEM_BYTES = 56 * 1024 * 1024


def swap(value, axis, stride):
    size = lax.axis_size(axis)
    return lax.ppermute(value, axis, [(a, a ^ stride) for a in range(size)])


class Lane:
    def __init__(self, depth):
        self.depth = depth
        self.sent = []

    def swap(self, value, axis, stride):
        if len(self.sent) >= self.depth:
            value, _ = lax.optimization_barrier((value, self.sent[-self.depth]))
        result = swap(value, axis, stride)
        self.sent.append(result)
        return result


def ordered(value, axis, strides):
    position = lax.axis_index(axis)
    for stride in strides:
        other = swap(value, axis, stride)
        high = (position // stride) % 2 == 1
        value = jnp.concatenate([jnp.where(high, other, value), jnp.where(high, value, other)], 0)
    return value


def contract(a, b, a_dim, b_dim):
    return lax.dot_general(a, b, (((a_dim,), (b_dim,)), ((), ())), preferred_element_type=jnp.float32)


def products_kernel(count, resume, finish, blocks, total_tokens, starts_ref, *refs):
    rows_ref, mix_ref, right_ref = refs[:3]
    pieces = refs[3 : 3 + count]
    rest = refs[3 + count :]
    if resume:
        residual = rest[0][...]
        rest = rest[1:]
    else:
        residual = contract(mix_ref[...], right_ref[...], 1, 0)
    for index in range(count):
        depth = pieces[index].shape[0]
        start = pl.multiple_of(starts_ref[index] * depth, depth)
        residual = residual - contract(rows_ref[:, pl.ds(start, depth)], pieces[index][...], 1, 0)
    if not finish:
        rest[0][...] = residual
        return
    right_out, left_out, loss_out = rest
    columns = right_ref.shape[1]
    mids = right_ref.shape[0] // blocks
    features = rows_ref.shape[1]
    in_size = features // mids

    @pl.when(pl.program_id(0) == 0)
    def _():
        right_out[...] = jnp.zeros_like(right_out)
        left_out[...] = jnp.zeros_like(left_out)
        loss_out[...] = jnp.zeros_like(loss_out)

    loss_out[...] += jnp.sum(residual * residual, axis=0, keepdims=True)
    slope = (residual / total_tokens).astype(jnp.bfloat16)
    full_right = contract(mix_ref[...], slope, 0, 0)
    column_block = lax.broadcasted_iota(jnp.int32, (mids, columns), 1) // (columns // blocks)
    grad_right = jnp.zeros((mids, columns), jnp.float32)
    for b in range(blocks):
        grad_right = jnp.where(column_block == b, full_right[b * mids : (b + 1) * mids], grad_right)
    right_out[...] += grad_right
    back_mix = contract(slope, right_ref[...], 1, 1).astype(jnp.bfloat16)
    span = min(features, 1024)
    for at in range(0, features, span):
        full_left = contract(back_mix, rows_ref[:, at : at + span], 0, 0)
        feature_block = (lax.broadcasted_iota(jnp.int32, (mids, span), 1) + at) // in_size
        same = lax.broadcasted_iota(jnp.int32, (mids, span), 0) == feature_block
        for b in range(blocks):
            part = jnp.where(same, full_left[b * mids : (b + 1) * mids], 0.0)
            left_out[b : b + 1, at : at + span] += jnp.sum(part, axis=0, keepdims=True)


def products(rows, mix, right_diag, pieces, starts, blocks, total_tokens, partial=None, finish=True):
    count = len(pieces)
    tokens, features = rows.shape
    mid_columns, columns = right_diag.shape
    steps = 1 if tokens <= 480 else 2
    tile = tokens // steps
    whole = lambda shape: pl.BlockSpec(shape, lambda t, starts: (0, 0))
    tiled = lambda width: pl.BlockSpec((tile, width), lambda t, starts: (t, 0))
    operands = [rows, mix, right_diag, *pieces]
    in_specs = [tiled(features), tiled(mid_columns), whole(right_diag.shape), *[whole(p.shape) for p in pieces]]
    if partial is not None:
        operands.append(partial)
        in_specs.append(tiled(columns))
    if finish:
        shapes = [(mid_columns // blocks, columns), (blocks, features), (1, columns)]
        out_specs = [whole(shape) for shape in shapes]
    else:
        shapes = [(tokens, columns)]
        out_specs = [tiled(columns)]
    depth = sum(p.shape[0] for p in pieces)
    flops = 2 * tokens * columns * (depth + 2 * mid_columns) + 2 * tokens * mid_columns * features
    results = pl.pallas_call(
        functools.partial(products_kernel, count, partial is not None, finish, blocks, total_tokens),
        out_shape=[jax.ShapeDtypeStruct(shape, jnp.float32) for shape in shapes],
        grid_spec=pltpu.PrefetchScalarGridSpec(
            num_scalar_prefetch=1, grid=(steps,), in_specs=in_specs, out_specs=out_specs
        ),
        compiler_params=pltpu.CompilerParams(vmem_limit_bytes=VMEM_BYTES),
        cost_estimate=pl.CostEstimate(
            flops=flops, bytes_accessed=2 * (tokens * features + depth * columns), transcendentals=0
        ),
    )(starts, *operands)
    return results if finish else results[0]


def local(tokens, dense_weight, left_factor, right_factor):
    tok_rows, features = tokens.shape
    weight_rows, columns = dense_weight.shape
    dp_count = lax.axis_size("dp")
    tensor_count = lax.axis_size("tensor")
    dp_pos = lax.axis_index("dp")
    tensor_pos = lax.axis_index("tensor")
    in_size = left_factor.shape[0]
    mids = right_factor.shape[0]
    blocks = left_factor.shape[1] * tensor_count // mids
    own_blocks = blocks // tensor_count
    out_size = columns // own_blocks
    total_tokens = tok_rows * dp_count

    bits = dp_count.bit_length() - 1
    strides = [1 << b for b in range(bits)]
    grouped = max(bits - 3, 0)
    pair = strides[grouped:][len(strides[grouped:]) // 2]
    others = [s for s in reversed(strides[grouped:]) if s != pair]
    pair_bit = (dp_pos // pair) % 2
    unit_rows = weight_rows << grouped

    half_blocks = own_blocks // 2
    chunks = 2 if half_blocks % 2 == 0 else 1
    chunk_blocks = half_blocks // chunks
    chunk_columns = chunk_blocks * out_size
    half_columns = half_blocks * out_size

    def weight_piece(half, chunk):
        start = half * half_columns + chunk * chunk_columns
        return lax.dynamic_slice_in_dim(dense_weight, start, chunk_columns, 1)

    held = [{} for _ in range(chunks)]
    theirs = []
    for chunk in range(chunks):
        held[chunk][0] = ordered(weight_piece(pair_bit, chunk), "dp", strides[:grouped])
        theirs.append(ordered(weight_piece(1 - pair_bit, chunk), "dp", strides[:grouped]))
    far, near = others
    far_lane, near_lane, pair_lane = Lane(2), Lane(2), Lane(1)

    def send(lane, stride, chunk, mask):
        held[chunk][mask ^ stride] = lane.swap(held[chunk][mask], "dp", stride)

    share = tok_rows // tensor_count
    late = max(16, (share // 4 + 8) // 16 * 16)
    token_parts = [(0, share - late), (share - late, late)]

    def fetch_tokens(which):
        begin, size = token_parts[which]
        part = lax.dynamic_slice_in_dim(tokens, tensor_pos * share + begin, size, 0)
        part = pair_lane.swap(part, "dp", pair)
        stride = tensor_count // 2
        while stride:
            part = jnp.concatenate([part, swap(part, "tensor", stride)], 0)
            stride //= 2
        return part

    last = chunks - 1
    held[0][pair] = pair_lane.swap(theirs[0], "dp", pair)
    send(far_lane, far, 0, 0)
    for chunk in range(chunks):
        send(near_lane, near, chunk, 0)
    send(far_lane, far, 0, pair)
    send(near_lane, near, 0, pair)
    send(near_lane, near, 0, far)
    early_rows = fetch_tokens(0)
    if last:
        held[last][pair] = pair_lane.swap(theirs[last], "dp", pair)
        send(far_lane, far, last, 0)
        send(far_lane, far, last, pair)
    send(near_lane, near, 0, far ^ pair)
    late_rows = fetch_tokens(1)
    if last:
        send(near_lane, near, last, pair)
        send(near_lane, near, last, far)
        send(near_lane, near, last, far ^ pair)

    left_blocks = left_factor.reshape(in_size, mids // tensor_count, blocks)
    left_blocks = lax.all_to_all(left_blocks, "tensor", split_axis=2, concat_axis=1, tiled=True)
    left_blocks = lax.dynamic_slice_in_dim(left_blocks, pair_bit * half_blocks, half_blocks, 2)
    eye_left = jnp.eye(mids, dtype=jnp.bfloat16)
    left_rows = left_blocks.transpose(1, 0, 2)
    left_diag = (left_rows[:, :, :, None] * eye_left[:, None, None, :]).reshape(features, half_blocks * mids)
    right_half = lax.dynamic_slice_in_dim(right_factor, pair_bit * half_columns, half_columns, 1)

    row_block = jnp.arange(chunk_blocks * mids) // mids
    column_block = jnp.arange(chunk_columns) // out_size
    same_block = row_block[:, None] == column_block[None, :]

    token_sets = (tokens, early_rows, late_rows)
    mixes = [
        jnp.dot(rows, left_diag, preferred_element_type=jnp.float32).astype(jnp.bfloat16) for rows in token_sets
    ]
    late_masks = (far ^ pair, far ^ pair ^ near)
    order = sorted(held[0], key=lambda mask: mask in late_masks)

    loss_part = jnp.zeros((), jnp.float32)
    right_parts, left_parts = [], []
    for chunk in range(chunks):
        right_chunk = right_half[:, chunk * chunk_columns : (chunk + 1) * chunk_columns]
        right_diag = jnp.where(same_block, jnp.tile(right_chunk, (chunk_blocks, 1)), jnp.bfloat16(0))
        sums = None
        for which, (rows, mix) in enumerate(zip(token_sets, mixes)):
            mix_chunk = mix[:, chunk * chunk_blocks * mids : (chunk + 1) * chunk_blocks * mids]
            pieces = [held[chunk][mask] for mask in order]
            starts = jnp.stack([(dp_pos ^ mask) >> grouped for mask in order]).astype(jnp.int32)
            call = functools.partial(products, rows, mix_chunk, right_diag, blocks=chunk_blocks, total_tokens=total_tokens)
            if which < 2 and chunk == last:
                cut = len(order) - 2
                partial = call(pieces=pieces[:cut], starts=starts[:cut], finish=False)
                terms = call(pieces=pieces[cut:], starts=starts[cut:], partial=partial)
            else:
                terms = call(pieces=pieces, starts=starts)
            sums = terms if sums is None else [a + b for a, b in zip(sums, terms)]
        right_parts.append(sums[0])
        left_parts.append(sums[1])
        loss_part = loss_part + jnp.sum(sums[2])

    left_sum = jnp.concatenate(left_parts, 0).reshape(half_blocks, mids, in_size).transpose(2, 0, 1)
    both = jnp.concatenate([*right_parts, left_sum.reshape(in_size, half_blocks * mids)], 1)
    width = both.shape[1]
    both = both.reshape((2,) * bits + (both.shape[0] // dp_count, width))
    order = [s for s in reversed(strides)]
    for stride in [near, far] + strides[:grouped]:
        at = order.index(stride)
        bit = (dp_pos // stride) % 2
        away = lax.dynamic_index_in_dim(both, 1 - bit, at, keepdims=False)
        kept = lax.dynamic_index_in_dim(both, bit, at, keepdims=False)
        both = kept + swap(away, "dp", stride)
        order.remove(stride)

    squares = both * both
    scalars = jnp.stack([jnp.sum(squares[..., half_columns:]), jnp.sum(squares[..., :half_columns]), loss_part])
    devices = dp_count * tensor_count
    scalars = jnp.broadcast_to(scalars[None], (devices, 3))
    sq_left, sq_right, loss_all = jnp.sum(lax.all_to_all(scalars, ("dp", "tensor"), 0, 0, tiled=True), 0)

    away = lax.dynamic_index_in_dim(both, 1 - pair_bit, 0, keepdims=False)
    kept = lax.dynamic_index_in_dim(both, pair_bit, 0, keepdims=False)
    other = swap(away, "dp", pair)
    low = jnp.where(pair_bit == 0, kept, other)
    high = jnp.where(pair_bit == 0, other, kept)
    right_rows = jnp.concatenate([low[:, :half_columns], high[:, :half_columns]], 1)
    left_low = low[:, half_columns:].reshape(-1, half_blocks, mids)
    left_high = high[:, half_columns:].reshape(-1, half_blocks, mids)
    left_rows = jnp.concatenate([left_low, left_high], 1)
    left_rows = lax.all_to_all(left_rows, "tensor", split_axis=2, concat_axis=1, tiled=True)
    left_rows = left_rows.transpose(0, 2, 1).reshape(left_rows.shape[0], -1)
    dir_left = left_rows * lax.rsqrt(sq_left / (features * blocks) + epsilon)
    dir_right = right_rows * lax.rsqrt(sq_right / (mids * columns * tensor_count) + epsilon)
    loss = loss_all / (2.0 * total_tokens)
    return (dir_left, dir_right, loss)


def solution(mesh):
    in_specs = (P("dp", None), P("dp", "tensor"), P(None, "tensor"), P(None, "tensor"))
    out_specs = (P("dp", "tensor"), P("dp", "tensor"), P())
    return jax.shard_map(local, mesh=mesh, in_specs=in_specs, out_specs=out_specs, check_vma=False)
```

time: 549 us -> 364 us (0.66)
  matrix products: 201 us -> 15.6 us
  Pallas kernels: 0 us -> 102 us
  waiting for transfers between devices: 207 us -> 137 us
  blocking collectives: 39.2 us -> 0 us
  starting transfers between devices: 29.8 us -> 40 us
    dot_general x44 -> x0, matrix products: 189 us -> none  [the longest x32 134 us: local(): jnp.dot(some, piece, preferred_element_type=jnp.float32)]
    pallas_call x0 -> x8, Pallas kernels: none -> 102 us  [products(): pl.pallas_call(functools.partial(products_kernel, count, partial is not N...]
    ppermute x20 -> x23, waiting for transfers between devices: 205 us -> 128 us  [swap(): return lax.ppermute(value, axis, [(a, a ^ stride) for a in range(size)])]
    psum x1 -> x0, blocking collectives: 39.2 us -> none  [local(): lax.psum((jnp.sum(left_rows * left_rows), jnp.sum(right_rows * right_rows...]
    ppermute x20 -> x23, starting transfers between devices: 22.7 us -> 29 us  [swap(): return lax.ppermute(value, axis, [(a, a ^ stride) for a in range(size)])]
    select_n x4 -> x1, other arithmetic: 6.26 us -> 0.02 us  [local(): low = jnp.where(pair_bit == 0, kept, other)]
    dot_general x2 -> x3, matrix products: 12.8 us -> 15.6 us  [local(): jnp.dot(rows, left_diag, preferred_element_type=jnp.float32)]
  transfers between devices with their start and end apart: 22 -> 26, of which waited for: 11 -> 12; matrix products, arithmetic and copies ran while one was open for 25% -> 13% of each run, Pallas kernels for 0% -> 18%
where the time goes in v2:
time: 364 us; the launch traced here: 357 us
  waiting for transfers between devices  137 us (38%)
  Pallas kernels  102 us (28%)
  starting transfers between devices  40 us (11%)
  local copies, waits for them, and re-layouts  39.3 us (11%)
  other arithmetic  17.4 us (5%)
  matrix products  15.6 us (4%)
  between operations  6.3 us (2%)
    ppermute x23, waiting for transfers between devices, swap(): return lax.ppermute(value, axis, [(a, a ^ stride) for a in range(size)])  128 us
    pallas_call x8, Pallas kernels, products(): pl.pallas_call(functools.partial(products_kernel, count, partial is not N...  102 us
    ppermute x23, starting transfers between devices, swap(): return lax.ppermute(value, axis, [(a, a ^ stride) for a in range(size)])  29 us
    dot_general x3, matrix products, local(): jnp.dot(rows, left_diag, preferred_element_type=jnp.float32)  15.6 us
    mul x1, local copies, waits for them, and re-layouts, local(): left_rows[:, :, :, None] * eye_left[:, None, None, :]  11.8 us
  transfers between devices with their start and end apart: 26, of which 12 were waited for; matrix products, arithmetic and copies ran while one was open for 13% of the time, Pallas kernels for 18%

profile of v2, /device:TPU:0, one launch (start us, length us, event | category | flops | bytes accessed | tf_op | source)
XLA Modules:
  0.0 357.1 jit_solution(1543660845578727010)
XLA Ops:
  0.7 3.6 %constant_dynamic-slice_fusion.6 = (bf16[512,896]{1,0:T(8,128)(2,1)}, bf16[512,896]{1,0:T(8,128)(2,1)S(1)}, bf16[512,896]{1,0:T(8,128)(2,1)}, bf16[512,896]{1,0:T(8,128)(2,1)S(1)}) fusion(bf16[512,3584]{1,0:T(8,128)(2,1)} %param.5, s32[]{:T(128)S(6)} %select_n.113, s32[]{:T(128)S(6)} %select_n.115, s32[]{:T(128)S(6)} %select_n.119, s32[]{:T(128)S(6)} %select_n.116), kind=kLoop, calls=%fused_computation.50 | loop fusion | bytes 7340048 | tf_op jit(solution)/shard_map/dynamic_slice | solution.py:157
  4.3 2.9 collective-permute-start.2
  7.3 2.6 collective-permute-start.1
  9.9 1.6 collective-permute-start
  12.0 0.9 reshape.100
  12.9 3.3 all-to-all-start
  17.5 0.7 stack.38.starts_ref
  18.2 1.9 constant_dynamic-slice_fusion.2
  20.1 1.2 compare_select_fusion.1
  21.3 2.6 constant_dynamic-slice_fusion.3
  25.3 23.8 %collective-permute-done.refs_4_ = bf16[512,896]{1,0:T(8,128)(2,1)} collective-permute-done((bf16[512,896]{1,0:T(8,128)(2,1)S(1)}, bf16[512,896]{1,0:T(8,128)(2,1)}, u32[]{:S(2)}, u32[]{:S(2)}) %collective-permute-start) | collective-permute-done | bytes 917536 | tf_op jit(solution)/shard_map/ppermute | solution.py:16
  49.1 2.6 collective-permute-start.8
  52.2 7.0 %broadcast_multiply_fusion = bf16[64,64,8,64]{3,2,1,0:T(8,128)(2,1)} fusion(bf16[64,64]{1,0:T(8,128)(2,1)S(1)} %fusion.1, bf16[64,64,8]{2,1,0:T(8,128)(2,1)S(1)} %copy.44), kind=kLoop, calls=%fused_computation | loop fusion | flops 2097152 | bytes 4268032 | tf_op jit(solution)/shard_map/mul | solution.py:209
  59.3 11.8 %mul.64 = bf16[4096,512]{1,0:T(8,128)(2,1)} reshape(bf16[64,64,8,64]{3,2,1,0:T(8,128)(2,1)} %broadcast_multiply_fusion) | data formatting | bytes 8388608 | tf_op jit(solution)/shard_map/mul | solution.py:209
  71.1 1.6 collective-permute-start.5
  72.7 2.9 collective-permute-start.18
  75.6 28.2 %collective-permute-done.6.refs_9_ = bf16[512,896]{1,0:T(8,128)(2,1)} collective-permute-done((bf16[512,896]{1,0:T(8,128)(2,1)}, bf16[512,896]{1,0:T(8,128)(2,1)}, u32[]{:S(2)}, u32[]{:S(2)}) %collective-permute-start.6) | collective-permute-done | bytes 917536 | tf_op jit(solution)/shard_map/ppermute | solution.py:16
  104.3 7.3 %collective-permute-done.8 = bf16[176,4096]{1,0:T(8,128)(2,1)S(1)} collective-permute-done((bf16[176,4096]{1,0:T(8,128)(2,1)}, bf16[176,4096]{1,0:T(8,128)(2,1)S(1)}, u32[]{:S(2)}, u32[]{:S(2)}) %collective-permute-start.8) | collective-permute-done | bytes 1441824 | tf_op jit(solution)/shard_map/ppermute | solution.py:16
  111.6 8.6 %fusion = bf16[960,512]{1,0:T(8,128)(2,1)S(1)} fusion(bf16[960,4096]{1,0:T(8,128)(2,1)} %refs_0_.5, bf16[4096,512]{1,0:T(8,128)(2,1)} %mul.64), kind=kOutput, calls=%fused_computation.4 | convolution fusion | flops 4027023360 | bytes 13041664 | tf_op jit(solution)/shard_map/dot_general | solution.py:218
  120.2 1.6 collective-permute-start.9
  121.8 1.1 fusion.6
  122.9 1.2 constant_dynamic-update-slice_fusion.2
  124.1 9.0 %collective-permute-done.18.refs_5_ = bf16[512,896]{1,0:T(8,128)(2,1)S(1)} collective-permute-done((bf16[512,896]{1,0:T(8,128)(2,1)S(1)}, bf16[512,896]{1,0:T(8,128)(2,1)S(1)}, u32[]{:S(2)}, u32[]{:S(2)}) %collective-permute-start.18) | collective-permute-done | bytes 917536 | tf_op jit(solution)/shard_map/ppermute | solution.py:16
  133.1 1.3 collective-permute-start.19
  134.4 7.7 %collective-permute-done.11.refs_4_ = bf16[512,896]{1,0:T(8,128)(2,1)S(1)} collective-permute-done((bf16[512,896]{1,0:T(8,128)(2,1)}, bf16[512,896]{1,0:T(8,128)(2,1)S(1)}, u32[]{:S(2)}, u32[]{:S(2)}) %collective-permute-start.11) | collective-permute-done | bytes 917536 | tf_op jit(solution)/shard_map/ppermute | solution.py:16
  142.1 1.0 collective-permute-start.12
  143.1 0.9 copy-done.4
  144.0 20.2 %shard_map.67 = (f32[64,896]{1,0:T(8,128)}, f32[4,4096]{1,0:T(4,128)}, f32[1,896]{1,0:T(1,128)}) custom-call(s32[8]{0:T(128)} %stack.38.starts_ref, bf16[960,4096]{1,0:T(8,128)(2,1)} %refs_0_.5, bf16[960,256]{1,0:T(8,128)(2,1)} %get-tuple-element.67.refs_1_, bf16[256,896]{1,0:T(8,128)(2,1)} %get-tuple-element.77.refs_2_, ...), custom_call_target="tpu_custom_call" | custom-call | flops 9940500480 | bytes 15204352 | tf_op jit(solution)/shard_map/pallas_call | solution.py:113
  164.9 2.1 collective-permute-start.15
  167.0 1.8 pad_maximum_fusion
  168.8 1.5 collective-permute-start.13
  170.3 1.4 constant_dynamic-update-slice_fusion.1
  171.7 12.4 %collective-permute-done.16.refs_7_ = bf16[512,896]{1,0:T(8,128)(2,1)S(1)} collective-permute-done((bf16[512,896]{1,0:T(8,128)(2,1)S(1)}, bf16[512,896]{1,0:T(8,128)(2,1)S(1)}, u32[]{:S(2)}, u32[]{:S(2)}) %collective-permute-start.16) | collective-permute-done | bytes 917536 | tf_op jit(solution)/shard_map/ppermute | solution.py:16
  184.1 20.9 %collective-permute-done.15.refs_3_.refs_9_ = bf16[512,896]{1,0:T(8,128)(2,1)} collective-permute-done((bf16[512,896]{1,0:T(8,128)(2,1)S(1)}, bf16[512,896]{1,0:T(8,128)(2,1)}, u32[]{:S(2)}, u32[]{:S(2)}) %collective-permute-start.15) | collective-permute-done | bytes 917536 | tf_op jit(solution)/shard_map/ppermute | solution.py:16
  205.1 1.5 collective-permute-start.17
  206.7 12.9 %shard_map.70.refs_5_ = f32[960,896]{1,0:T(8,128)} custom-call(s32[6]{0:T(128)} %stack.40.starts_ref, bf16[960,4096]{1,0:T(8,128)(2,1)} %refs_0_.5, bf16[960,256]{1,0:T(8,128)(2,1)} %get-tuple-element.68.refs_1_, bf16[256,896]{1,0:T(8,128)(2,1)} %get-tuple-element.78.refs_2_, bf16[512,896]{1,0:T(8,128)(2,1)} %copy-done.2, bf16[512,896]{1,0:T(8,128)(2,1)} %copy-done.6, ...), custom_call_target="tpu_custom_call" | custom-call | flops 8178892800 | bytes 13369344 | tf_op jit(solution)/shard_map/pallas_call | solution.py:113
  219.7 7.3 %collective-permute-done.17.refs_4_.refs_10_ = bf16[512,896]{1,0:T(8,128)(2,1)} collective-permute-done((bf16[512,896]{1,0:T(8,128)(2,1)}, bf16[512,896]{1,0:T(8,128)(2,1)}, u32[]{:S(2)}, u32[]{:S(2)}) %collective-permute-start.17) | collective-permute-done | bytes 917536 | tf_op jit(solution)/shard_map/ppermute | solution.py:16
  226.9 12.4 %shard_map.71 = (f32[64,896]{1,0:T(8,128)}, f32[4,4096]{1,0:T(4,128)}, f32[1,896]{1,0:T(1,128)}) custom-call(s32[2]{0:T(128)} %pad_add_fusion.starts_ref, bf16[960,4096]{1,0:T(8,128)(2,1)} %refs_0_.5, bf16[960,256]{1,0:T(8,128)(2,1)} %get-tuple-element.68.refs_1_, bf16[256,896]{1,0:T(8,128)(2,1)} %get-tuple-element.78.refs_2_, ...), custom_call_target="tpu_custom_call" | custom-call | flops 4655677440 | bytes 9699328 | tf_op jit(solution)/shard_map/pallas_call | solution.py:113
  239.3 1.3 constant_dynamic-update-slice_fusion.3.refs_0_
  240.7 1.2 convolution_convert_fusion.2
  241.9 0.7 fusion.8
  242.6 9.1 %shard_map.69 = (f32[64,896]{1,0:T(8,128)}, f32[4,4096]{1,0:T(4,128)}, f32[1,896]{1,0:T(1,128)}) custom-call(s32[8]{0:T(128)} %stack.38.starts_ref, bf16[256,4096]{1,0:T(8,128)(2,1)} %copy-done, bf16[256,256]{1,0:T(8,128)(2,1)} %get-tuple-element.73.refs_1_, bf16[256,896]{1,0:T(8,128)(2,1)} %get-tuple-element.77.refs_2_, ...), custom_call_target="tpu_custom_call" | custom-call | flops 2650800128 | bytes 9437184 | tf_op jit(solution)/shard_map/pallas_call | solution.py:113
  251.8 9.1 %shard_map.74 = (f32[64,896]{1,0:T(8,128)}, f32[4,4096]{1,0:T(4,128)}, f32[1,896]{1,0:T(1,128)}) custom-call(s32[8]{0:T(128)} %stack.38.starts_ref, bf16[256,4096]{1,0:T(8,128)(2,1)} %copy-done, bf16[256,256]{1,0:T(8,128)(2,1)} %get-tuple-element.74.refs_1_, bf16[256,896]{1,0:T(8,128)(2,1)} %get-tuple-element.78.refs_2_, bf16[512,896]{1,0:T(8,128)(2,1)} %copy-done.2, ...), custom_call_target="tpu_custom_call" | custom-call | flops 2650800128 | bytes 9437184 | tf_op jit(solution)/shard_map/pallas_call | solution.py:113
  260.9 3.7 %constant_dynamic-update-slice_fusion.refs_0_ = bf16[704,4096]{1,0:T(8,128)(2,1)} fusion(bf16[704,4096]{1,0:T(8,128)(2,1)} %constant_dynamic-update-slice_fusion.1, bf16[352,4096]{1,0:T(8,128)(2,1)} %collective-permute-done.10), kind=kLoop, calls=%fused_computation.31 | loop fusion | bytes 5767168 | tf_op jit(solution)/shard_map/concatenate | solution.py:180
  264.6 5.8 %convolution_convert_fusion.1 = bf16[704,512]{1,0:T(8,128)(2,1)S(1)} fusion(bf16[704,4096]{1,0:T(8,128)(2,1)} %constant_dynamic-update-slice_fusion.refs_0_, bf16[4096,512]{1,0:T(8,128)(2,1)S(1)} %copy-done.1), kind=kOutput, calls=%fused_computation.3 | convolution fusion | flops 2953150464 | bytes 10682368 | tf_op jit(solution)/shard_map/dot_general | solution.py:218
  270.4 0.9 fusion.7
  271.3 16.9 %shard_map.68 = (f32[64,896]{1,0:T(8,128)}, f32[4,4096]{1,0:T(4,128)}, f32[1,896]{1,0:T(1,128)}) custom-call(s32[8]{0:T(128)} %stack.38.starts_ref, bf16[704,4096]{1,0:T(8,128)(2,1)} %constant_dynamic-update-slice_fusion.refs_0_, bf16[704,256]{1,0:T(8,128)(2,1)} %get-tuple-element.69.refs_1_, bf16[256,896]{1,0:T(8,128)(2,1)} %get-tuple-element.77.refs_2_, ...), custom_call_target="tpu_custom_call" | custom-call | flops 7289700352 | bytes 13107200 | tf_op jit(solution)/shard_map/pallas_call | solution.py:113
  288.2 10.6 %shard_map.72.refs_5_ = f32[704,896]{1,0:T(8,128)} custom-call(s32[6]{0:T(128)} %stack.40.starts_ref, bf16[704,4096]{1,0:T(8,128)(2,1)} %constant_dynamic-update-slice_fusion.refs_0_, bf16[704,256]{1,0:T(8,128)(2,1)} %get-tuple-element.70.refs_1_, bf16[256,896]{1,0:T(8,128)(2,1)} %get-tuple-element.78.refs_2_, bf16[512,896]{1,0:T(8,128)(2,1)} %copy-done.2, ...), custom_call_target="tpu_custom_call" | custom-call | flops 5997854720 | bytes 11272192 | tf_op jit(solution)/shard_map/pallas_call | solution.py:113
  298.9 10.6 %shard_map.73 = (f32[64,896]{1,0:T(8,128)}, f32[4,4096]{1,0:T(4,128)}, f32[1,896]{1,0:T(1,128)}) custom-call(s32[2]{0:T(128)} %pad_add_fusion.starts_ref, bf16[704,4096]{1,0:T(8,128)(2,1)} %constant_dynamic-update-slice_fusion.refs_0_, bf16[704,256]{1,0:T(8,128)(2,1)} %get-tuple-element.70.refs_1_, bf16[256,896]{1,0:T(8,128)(2,1)} %get-tuple-element.78.refs_2_, ...), custom_call_target="tpu_custom_call" | custom-call | flops 3414163456 | bytes 7602176 | tf_op jit(solution)/shard_map/pallas_call | solution.py:113
  309.6 0.9 add_add_fusion.2
  311.0 1.0 add_add_fusion
  312.1 1.6 collective-permute-start.20
  313.6 5.8 %collective-permute-done.20 = f32[2,2,8,2304]{3,2,1,0:T(8,128)S(1)} collective-permute-done((f32[2,2,8,2304]{3,2,1,0:T(8,128)S(1)}, f32[2,2,8,2304]{3,2,1,0:T(8,128)S(1)}, u32[]{:S(2)}, u32[]{:S(2)}) %collective-permute-start.20) | collective-permute-done | bytes 294944 | tf_op jit(solution)/shard_map/ppermute | solution.py:16
  321.6 5.6 %collective-permute-done.21 = f32[2,8,2304]{2,1,0:T(8,128)S(1)} collective-permute-done((f32[2,8,2304]{2,1,0:T(8,128)S(1)}, f32[2,8,2304]{2,1,0:T(8,128)S(1)}, u32[]{:S(2)}, u32[]{:S(2)}) %collective-permute-start.21) | collective-permute-done | bytes 147488 | tf_op jit(solution)/shard_map/ppermute | solution.py:16
  328.5 1.4 pad_maximum_fusion.5
  330.4 4.5 %all-to-all-start.2 = ((f32[32,1,3]{2,1,0:T(1,128)}), f32[32,1,3]{2,1,0:T(1,128)S(1)}, u32[]{:S(2)}, u32[]{:S(2)}) async-start(f32[32,1,3]{2,1,0:T(1,128)} %broadcast_in_dim.8), calls=%async_computation.2 | async-start | bytes 32768 | tf_op jit(solution)/shard_map/all_to_all | solution.py:262
  335.0 1.8 collective-permute-start.22
  336.8 5.3 %all-to-all-done.2 = f32[32,1,3]{2,1,0:T(1,128)S(1)} async-done(((f32[32,1,3]{2,1,0:T(1,128)}), f32[32,1,3]{2,1,0:T(1,128)S(1)}, u32[]{:S(2)}, u32[]{:S(2)}) %all-to-all-start.2) | async-done | bytes 416 | tf_op jit(solution)/shard_map/all_to_all | solution.py:262
  345.2 0.8 reshape.102
  345.9 3.3 all-to-all-start.1
  349.2 0.7 maximum_multiply_fusion
  349.9 3.3 all-to-all-done.1
  353.6 0.7 reduce.1
  354.9 0.7 mul.74
  (122 shorter events, 10.3 us)
Async XLA Ops:
  0.6 10.8 %copy-start.14 = (bf16[64,1024]{1,0:T(8,128)(2,1)S(1)}, bf16[64,1024]{1,0:T(8,128)(2,1)}, u32[]{:S(2)}) copy-start(bf16[64,1024]{1,0:T(8,128)(2,1)} %param.6) | copy-start | bytes 393220
  0.7 16.2 %copy-start.15 = (bf16[64,3584]{1,0:T(8,128)(2,1)S(1)}, bf16[64,3584]{1,0:T(8,128)(2,1)}, u32[]{:S(2)}) copy-start(bf16[64,3584]{1,0:T(8,128)(2,1)} %param.7) | copy-start | bytes 1376260
  4.3 68.3 %copy-start.2 = (bf16[512,896]{1,0:T(8,128)(2,1)}, bf16[512,896]{1,0:T(8,128)(2,1)S(1)}, u32[]{:S(2)}) copy-start(bf16[512,896]{1,0:T(8,128)(2,1)S(1)} %get-tuple-element.44.refs_3_) | copy-start | bytes 2752516
  4.3 47.4 %collective-permute-start.2 = (bf16[512,896]{1,0:T(8,128)(2,1)}, bf16[512,896]{1,0:T(8,128)(2,1)}, u32[]{:S(2)}, u32[]{:S(2)}) collective-permute-start(bf16[512,896]{1,0:T(8,128)(2,1)} %get-tuple-element.63.refs_3_), channel_id=1, source_target_pairs={{0,4},{4,0},{8,12},{12,8},{16,20},{20,16},{24,28},{28,24},{1,5},{5... | collective-permute-start | bytes 2752520 | tf_op jit(solution)/shard_map/ppermute | solution.py:16
  7.3 63.8 %collective-permute-start.1 = (bf16[512,896]{1,0:T(8,128)(2,1)}, bf16[512,896]{1,0:T(8,128)(2,1)}, u32[]{:S(2)}, u32[]{:S(2)}) collective-permute-start(bf16[512,896]{1,0:T(8,128)(2,1)} %get-tuple-element.63.refs_3_), channel_id=1, source_target_pairs={{0,16},{4,20},{8,24},{12,28},{16,0},{20,4},{24,8},{28,12},{1,17},{... | collective-permute-start | bytes 2752520 | tf_op jit(solution)/shard_map/ppermute | solution.py:16
  9.9 39.2 %collective-permute-start = (bf16[512,896]{1,0:T(8,128)(2,1)S(1)}, bf16[512,896]{1,0:T(8,128)(2,1)}, u32[]{:S(2)}, u32[]{:S(2)}) collective-permute-start(bf16[512,896]{1,0:T(8,128)(2,1)S(1)} %get-tuple-element.64), channel_id=1, source_target_pairs={{0,8},{4,12},{8,0},{12,4},{16,24},{20,28},{24,16},{28,20},{1,9},{5... | collective-permute-start | bytes 2752520 | tf_op jit(solution)/shard_map/ppermute | solution.py:16
  12.9 11.6 %all-to-all-start = ((bf16[4,2,8192]{2,1,0:T(2,128)(2,1)}), bf16[4,2,8192]{2,1,0:T(2,128)(2,1)S(1)}, u32[]{:S(2)}, u32[]{:S(2)}) async-start(bf16[4,2,8192]{2,1,0:T(2,128)(2,1)} %reshape.100), calls=%async_computation | async-start | bytes 262144 | tf_op jit(solution)/shard_map/all_to_all | solution.py:205
  16.2 54.9 %collective-permute-start.4 = (bf16[512,896]{1,0:T(8,128)(2,1)S(1)}, bf16[512,896]{1,0:T(8,128)(2,1)}, u32[]{:S(2)}, u32[]{:S(2)}) collective-permute-start(bf16[512,896]{1,0:T(8,128)(2,1)S(1)} %get-tuple-element.44.refs_3_), channel_id=1, source_target_pairs={{0,4},{4,0},{8,12},{12,8},{16,20},{20,16},{24,28},{28,24},{1,5},{5... | collective-permute-start | bytes 2752520 | tf_op jit(solution)/shard_map/ppermute | solution.py:16
  49.1 62.4 %collective-permute-start.8 = (bf16[176,4096]{1,0:T(8,128)(2,1)}, bf16[176,4096]{1,0:T(8,128)(2,1)S(1)}, u32[]{:S(2)}, u32[]{:S(2)}) collective-permute-start(bf16[176,4096]{1,0:T(8,128)(2,1)} %constant_dynamic-slice_fusion.3), channel_id=1, source_target_pairs={{0,8},{4,12},{8,0},{12,4},{16,24},{20,28},{24,16},{28,20},{1,9},{5... | collective-permute-start | bytes 4325384 | tf_op jit(solution)/shard_map/ppermute | solution.py:16
  51.7 23.9 %collective-permute-start.3 = (bf16[512,896]{1,0:T(8,128)(2,1)}, bf16[512,896]{1,0:T(8,128)(2,1)}, u32[]{:S(2)}, u32[]{:S(2)}) collective-permute-start(bf16[512,896]{1,0:T(8,128)(2,1)} %collective-permute-done.refs_4_), channel_id=1, source_target_pairs={{0,4},{4,0},{8,12},{12,8},{16,20},{20,16},{24,28},{28,24},{1,5},{5... | collective-permute-start | bytes 2752520 | tf_op jit(solution)/shard_map/ppermute | solution.py:16
  52.2 51.5 %collective-permute-start.6 = (bf16[512,896]{1,0:T(8,128)(2,1)}, bf16[512,896]{1,0:T(8,128)(2,1)}, u32[]{:S(2)}, u32[]{:S(2)}) collective-permute-start(bf16[512,896]{1,0:T(8,128)(2,1)} %collective-permute-done.refs_4_), channel_id=1, source_target_pairs={{0,16},{4,20},{8,24},{12,28},{16,0},{20,4},{24,8},{28,12},{1,17},{... | collective-permute-start | bytes 2752520 | tf_op jit(solution)/shard_map/ppermute | solution.py:16
  71.1 72.0 %collective-permute-start.5 = (bf16[512,896]{1,0:T(8,128)(2,1)}, bf16[512,896]{1,0:T(8,128)(2,1)S(1)}, u32[]{:S(2)}, u32[]{:S(2)}) collective-permute-start(bf16[512,896]{1,0:T(8,128)(2,1)} %collective-permute-done.1.refs_5_), channel_id=1, source_target_pairs={{0,4},{4,0},{8,12},{12,8},{16,20},{20,16},{24,28},{28,24},{1,5},{5... | collective-permute-start | bytes 2752520 | tf_op jit(solution)/shard_map/ppermute | solution.py:16
  72.7 60.4 %collective-permute-start.18 = (bf16[512,896]{1,0:T(8,128)(2,1)S(1)}, bf16[512,896]{1,0:T(8,128)(2,1)S(1)}, u32[]{:S(2)}, u32[]{:S(2)}) collective-permute-start(bf16[512,896]{1,0:T(8,128)(2,1)S(1)} %get-tuple-element.44.refs_3_), channel_id=1, source_target_pairs={{0,16},{4,20},{8,24},{12,28},{16,0},{20,4},{24,8},{28,12},{1,17},{... | collective-permute-start | bytes 2752520 | tf_op jit(solution)/shard_map/ppermute | solution.py:16
  103.8 29.3 %collective-permute-start.7 = (bf16[512,896]{1,0:T(8,128)(2,1)}, bf16[512,896]{1,0:T(8,128)(2,1)S(1)}, u32[]{:S(2)}, u32[]{:S(2)}) collective-permute-start(bf16[512,896]{1,0:T(8,128)(2,1)} %collective-permute-done.6.refs_9_), channel_id=1, source_target_pairs={{0,4},{4,0},{8,12},{12,8},{16,20},{20,16},{24,28},{28,24},{1,5},{5... | collective-permute-start | bytes 2752520 | tf_op jit(solution)/shard_map/ppermute | solution.py:16
  111.6 30.5 %collective-permute-start.11 = (bf16[512,896]{1,0:T(8,128)(2,1)}, bf16[512,896]{1,0:T(8,128)(2,1)S(1)}, u32[]{:S(2)}, u32[]{:S(2)}) collective-permute-start(bf16[512,896]{1,0:T(8,128)(2,1)} %get-tuple-element.38), channel_id=1, source_target_pairs={{0,8},{4,12},{8,0},{12,4},{16,24},{20,28},{24,16},{28,20},{1,9},{5... | collective-permute-start | bytes 2752520 | tf_op jit(solution)/shard_map/ppermute | solution.py:16
  120.2 46.8 %collective-permute-start.9 = (bf16[176,4096]{1,0:T(8,128)(2,1)S(1)}, bf16[176,4096]{1,0:T(8,128)(2,1)S(1)}, u32[]{:S(2)}, u32[]{:S(2)}) collective-permute-start(bf16[176,4096]{1,0:T(8,128)(2,1)S(1)} %collective-permute-done.8), channel_id=1, source_target_pairs={{0,2},{1,3},{2,0},{3,1},{4,6},{5,7},{6,4},{7,5},{8,10},{9,11},{10,... | collective-permute-start | bytes 4325384 | tf_op jit(solution)/shard_map/ppermute | solution.py:16
  133.0 31.2 %copy-start.3 = (bf16[512,896]{1,0:T(8,128)(2,1)}, bf16[512,896]{1,0:T(8,128)(2,1)S(1)}, u32[]{:S(2)}) copy-start(bf16[512,896]{1,0:T(8,128)(2,1)S(1)} %collective-permute-done.18.refs_5_) | copy-start | bytes 2752516
  133.1 10.0 %copy-start.5 = (bf16[512,896]{1,0:T(8,128)(2,1)}, bf16[512,896]{1,0:T(8,128)(2,1)S(1)}, u32[]{:S(2)}) copy-start(bf16[512,896]{1,0:T(8,128)(2,1)S(1)} %collective-permute-done.7.refs_10_) | copy-start | bytes 2752516
  133.1 73.7 %collective-permute-start.19 = (bf16[512,896]{1,0:T(8,128)(2,1)S(1)}, bf16[512,896]{1,0:T(8,128)(2,1)}, u32[]{:S(2)}, u32[]{:S(2)}) collective-permute-start(bf16[512,896]{1,0:T(8,128)(2,1)S(1)} %collective-permute-done.18.refs_5_), channel_id=1, source_target_pairs={{0,4},{4,0},{8,12},{12,8},{16,20},{20,16},{24,28},{28,24},{1,5},{5... | collective-permute-start | bytes 2752520 | tf_op jit(solution)/shard_map/ppermute | solution.py:16
  142.1 1.0 copy-start.6
  142.1 26.7 %collective-permute-start.12 = (bf16[64,4096]{1,0:T(8,128)(2,1)}, bf16[64,4096]{1,0:T(8,128)(2,1)S(1)}, u32[]{:S(2)}, u32[]{:S(2)}) collective-permute-start(bf16[64,4096]{1,0:T(8,128)(2,1)} %constant_dynamic-slice_fusion.2), channel_id=1, source_target_pairs={{0,8},{4,12},{8,0},{12,4},{16,24},{20,28},{24,16},{28,20},{1,9},{5... | collective-permute-start | bytes 1572872 | tf_op jit(solution)/shard_map/ppermute | solution.py:16
  143.1 0.9 copy-start.4
  144.0 20.2 %copy-start.7 = (bf16[512,896]{1,0:T(8,128)(2,1)S(1)}, bf16[512,896]{1,0:T(8,128)(2,1)}, u32[]{:S(2)}) copy-start(bf16[512,896]{1,0:T(8,128)(2,1)} %copy-done.6) | copy-start | bytes 2752516
  164.2 19.9 %collective-permute-start.16 = (bf16[512,896]{1,0:T(8,128)(2,1)S(1)}, bf16[512,896]{1,0:T(8,128)(2,1)S(1)}, u32[]{:S(2)}, u32[]{:S(2)}) collective-permute-start(bf16[512,896]{1,0:T(8,128)(2,1)S(1)} %copy-done.7), channel_id=1, source_target_pairs={{0,4},{4,0},{8,12},{12,8},{16,20},{20,16},{24,28},{28,24},{1,5},{5... | collective-permute-start | bytes 2752520 | tf_op jit(solution)/shard_map/ppermute | solution.py:16
  164.9 40.2 %collective-permute-start.15 = (bf16[512,896]{1,0:T(8,128)(2,1)S(1)}, bf16[512,896]{1,0:T(8,128)(2,1)}, u32[]{:S(2)}, u32[]{:S(2)}) collective-permute-start(bf16[512,896]{1,0:T(8,128)(2,1)S(1)} %copy-done.7), channel_id=1, source_target_pairs={{0,16},{4,20},{8,24},{12,28},{16,0},{20,4},{24,8},{28,12},{1,17},{... | collective-permute-start | bytes 2752520 | tf_op jit(solution)/shard_map/ppermute | solution.py:16
  168.8 92.1 %collective-permute-start.10 = (bf16[352,4096]{1,0:T(8,128)(2,1)}, bf16[352,4096]{1,0:T(8,128)(2,1)}, u32[]{:S(2)}, u32[]{:S(2)}) collective-permute-start(bf16[352,4096]{1,0:T(8,128)(2,1)} %pad_maximum_fusion), channel_id=1, source_target_pairs={{0,1},{1,0},{2,3},{3,2},{4,5},{5,4},{6,7},{7,6},{8,9},{9,8},{10,11... | collective-permute-start | bytes 8650760 | tf_op jit(solution)/shard_map/ppermute | solution.py:16
  168.8 37.8 %collective-permute-start.13 = (bf16[64,4096]{1,0:T(8,128)(2,1)S(1)}, bf16[64,4096]{1,0:T(8,128)(2,1)S(1)}, u32[]{:S(2)}, u32[]{:S(2)}) collective-permute-start(bf16[64,4096]{1,0:T(8,128)(2,1)S(1)} %collective-permute-done.12), channel_id=1, source_target_pairs={{0,2},{1,3},{2,0},{3,1},{4,6},{5,7},{6,4},{7,5},{8,10},{9,11},{10,... | collective-permute-start | bytes 1572872 | tf_op jit(solution)/shard_map/ppermute | solution.py:16
  184.1 22.6 %copy-start.8 = (bf16[512,896]{1,0:T(8,128)(2,1)}, bf16[512,896]{1,0:T(8,128)(2,1)S(1)}, u32[]{:S(2)}) copy-start(bf16[512,896]{1,0:T(8,128)(2,1)S(1)} %collective-permute-done.16.refs_7_) | copy-start | bytes 2752516
  205.1 21.9 %collective-permute-start.17 = (bf16[512,896]{1,0:T(8,128)(2,1)}, bf16[512,896]{1,0:T(8,128)(2,1)}, u32[]{:S(2)}, u32[]{:S(2)}) collective-permute-start(bf16[512,896]{1,0:T(8,128)(2,1)} %collective-permute-done.15.refs_3_.refs_9_), channel_id=1, source_target_pairs={{0,4},{4,0},{8,12},{12,8},{16,20},{20,16},{24,28},{28,24},{1,5},{5... | collective-permute-start | bytes 2752520 | tf_op jit(solution)/shard_map/ppermute | solution.py:16
  206.6 32.7 %collective-permute-start.14 = (bf16[128,4096]{1,0:T(8,128)(2,1)S(1)}, bf16[128,4096]{1,0:T(8,128)(2,1)}, u32[]{:S(2)}, u32[]{:S(2)}) collective-permute-start(bf16[128,4096]{1,0:T(8,128)(2,1)S(1)} %pad_maximum_fusion.1), channel_id=1, source_target_pairs={{0,1},{1,0},{2,3},{3,2},{4,5},{5,4},{6,7},{7,6},{8,9},{9,8},{10,11... | collective-permute-start | bytes 3145736 | tf_op jit(solution)/shard_map/ppermute | solution.py:16
  219.7 21.0 %copy-start.1 = (bf16[4096,512]{1,0:T(8,128)(2,1)S(1)}, bf16[4096,512]{1,0:T(8,128)(2,1)}, u32[]{:S(2)}) copy-start(bf16[4096,512]{1,0:T(8,128)(2,1)} %mul.64) | copy-start | bytes 12582916
  240.7 2.0 copy-start
  298.8 10.8 %copy-start.16 = (f32[4,4096]{1,0:T(4,128)S(1)}, f32[4,4096]{1,0:T(4,128)}, u32[]{:S(2)}) copy-start(f32[4,4096]{1,0:T(4,128)} %get-tuple-element.49) | copy-start | bytes 196612
  298.8 10.8 %copy-start.17 = (f32[4,4096]{1,0:T(4,128)S(1)}, f32[4,4096]{1,0:T(4,128)}, u32[]{:S(2)}) copy-start(f32[4,4096]{1,0:T(4,128)} %get-tuple-element.52) | copy-start | bytes 196612
  298.8 10.8 %copy-start.18 = (f32[4,4096]{1,0:T(4,128)S(1)}, f32[4,4096]{1,0:T(4,128)}, u32[]{:S(2)}) copy-start(f32[4,4096]{1,0:T(4,128)} %get-tuple-element.51) | copy-start | bytes 196612
  298.8 10.8 %copy-start.19 = (f32[4,4096]{1,0:T(4,128)S(1)}, f32[4,4096]{1,0:T(4,128)}, u32[]{:S(2)}) copy-start(f32[4,4096]{1,0:T(4,128)} %get-tuple-element.54) | copy-start | bytes 196612
  298.8 10.8 %copy-start.20 = (f32[4,4096]{1,0:T(4,128)S(1)}, f32[4,4096]{1,0:T(4,128)}, u32[]{:S(2)}) copy-start(f32[4,4096]{1,0:T(4,128)} %get-tuple-element.50) | copy-start | bytes 196612
  298.8 12.1 %copy-start.9 = (f32[64,896]{1,0:T(8,128)S(1)}, f32[64,896]{1,0:T(8,128)}, u32[]{:S(2)}) copy-start(f32[64,896]{1,0:T(8,128)} %get-tuple-element.35) | copy-start | bytes 688132
  298.8 12.1 %copy-start.11 = (f32[64,896]{1,0:T(8,128)S(1)}, f32[64,896]{1,0:T(8,128)}, u32[]{:S(2)}) copy-start(f32[64,896]{1,0:T(8,128)} %get-tuple-element.40) | copy-start | bytes 688132
  298.8 12.1 %copy-start.13 = (f32[64,896]{1,0:T(8,128)S(1)}, f32[64,896]{1,0:T(8,128)}, u32[]{:S(2)}) copy-start(f32[64,896]{1,0:T(8,128)} %get-tuple-element.37) | copy-start | bytes 688132
  298.9 12.1 %copy-start.10 = (f32[64,896]{1,0:T(8,128)S(1)}, f32[64,896]{1,0:T(8,128)}, u32[]{:S(2)}) copy-start(f32[64,896]{1,0:T(8,128)} %get-tuple-element.46) | copy-start | bytes 688132
  298.9 12.1 %copy-start.12 = (f32[64,896]{1,0:T(8,128)S(1)}, f32[64,896]{1,0:T(8,128)}, u32[]{:S(2)}) copy-start(f32[64,896]{1,0:T(8,128)} %get-tuple-element.48) | copy-start | bytes 688132
  309.5 10.1 %copy-start.21 = (f32[1,896]{1,0:T(1,128)S(1)}, f32[1,896]{1,0:T(1,128)}, u32[]{:S(2)}) copy-start(f32[1,896]{1,0:T(1,128)} %get-tuple-element.55) | copy-start | bytes 10756
  309.5 10.1 %copy-start.22 = (f32[1,896]{1,0:T(1,128)S(1)}, f32[1,896]{1,0:T(1,128)}, u32[]{:S(2)}) copy-start(f32[1,896]{1,0:T(1,128)} %get-tuple-element.58) | copy-start | bytes 10756
  309.5 10.1 %copy-start.23 = (f32[1,896]{1,0:T(1,128)S(1)}, f32[1,896]{1,0:T(1,128)}, u32[]{:S(2)}) copy-start(f32[1,896]{1,0:T(1,128)} %get-tuple-element.57) | copy-start | bytes 10756
  309.5 10.1 %copy-start.24 = (f32[1,896]{1,0:T(1,128)S(1)}, f32[1,896]{1,0:T(1,128)}, u32[]{:S(2)}) copy-start(f32[1,896]{1,0:T(1,128)} %get-tuple-element.60) | copy-start | bytes 10756
  309.6 10.1 %copy-start.25 = (f32[1,896]{1,0:T(1,128)S(1)}, f32[1,896]{1,0:T(1,128)}, u32[]{:S(2)}) copy-start(f32[1,896]{1,0:T(1,128)} %get-tuple-element.56) | copy-start | bytes 10756
  309.6 10.1 %copy-start.26 = (f32[1,896]{1,0:T(1,128)S(1)}, f32[1,896]{1,0:T(1,128)}, u32[]{:S(2)}) copy-start(f32[1,896]{1,0:T(1,128)} %get-tuple-element.59) | copy-start | bytes 10756
  312.1 7.4 %collective-permute-start.20 = (f32[2,2,8,2304]{3,2,1,0:T(8,128)S(1)}, f32[2,2,8,2304]{3,2,1,0:T(8,128)S(1)}, u32[]{:S(2)}, u32[]{:S(2)}) collective-permute-start(f32[2,2,8,2304]{3,2,1,0:T(8,128)S(1)} %dynamic-slice_bitcast_fusion), channel_id=1, source_target_pairs={{0,4},{4,0},{8,12},{12,8},{16,20},{20,16},{24,28},{28,24},{1,5},{5... | collective-permute-start | bytes 884744 | tf_op jit(solution)/shard_map/ppermute | solution.py:16
  319.5 7.7 %collective-permute-start.21 = (f32[2,8,2304]{2,1,0:T(8,128)S(1)}, f32[2,8,2304]{2,1,0:T(8,128)S(1)}, u32[]{:S(2)}, u32[]{:S(2)}) collective-permute-start(f32[2,8,2304]{2,1,0:T(8,128)S(1)} %dynamic-slice_bitcast_fusion.1), channel_id=1, source_target_pairs={{0,16},{4,20},{8,24},{12,28},{16,0},{20,4},{24,8},{28,12},{1,17},{... | collective-permute-start | bytes 442376 | tf_op jit(solution)/shard_map/ppermute | solution.py:16
  330.4 11.6 %all-to-all-start.2 = ((f32[32,1,3]{2,1,0:T(1,128)}), f32[32,1,3]{2,1,0:T(1,128)S(1)}, u32[]{:S(2)}, u32[]{:S(2)}) async-start(f32[32,1,3]{2,1,0:T(1,128)} %broadcast_in_dim.8), calls=%async_computation.2 | async-start | bytes 32768 | tf_op jit(solution)/shard_map/all_to_all | solution.py:262
  335.0 9.8 %collective-permute-start.22 = (f32[8,2304]{1,0:T(8,128)S(1)}, f32[8,2304]{1,0:T(8,128)S(1)}, u32[]{:S(2)}, u32[]{:S(2)}) collective-permute-start(f32[8,2304]{1,0:T(8,128)S(1)} %dynamic-slice_bitcast_fusion.3), channel_id=1, source_target_pairs={{0,8},{4,12},{8,0},{12,4},{16,24},{20,28},{24,16},{28,20},{1,9},{5... | collective-permute-start | bytes 221192 | tf_op jit(solution)/shard_map/ppermute | solution.py:16
  345.9 7.2 %all-to-all-start.1 = ((f32[4,1,2048]{2,1,0:T(1,128)}), f32[4,1,2048]{2,1,0:T(1,128)S(1)}, u32[]{:S(2)}, u32[]{:S(2)}) async-start(f32[4,1,2048]{2,1,0:T(1,128)} %reshape.102), calls=%async_computation.1 | async-start | bytes 65536 | tf_op jit(solution)/shard_map/all_to_all | solution.py:273

commit v3 on v1

v3 whole, which is shorter than its diff:
```python
import functools

import jax
import jax.numpy as jnp
from jax import lax
from jax.experimental import pallas as pl
from jax.experimental.pallas import tpu as pltpu
from jax.sharding import PartitionSpec as P

epsilon = 1e-06
VMEM_BYTES = 56 * 1024 * 1024


def swap(value, axis, stride):
    size = lax.axis_size(axis)
    return lax.ppermute(value, axis, [(a, a ^ stride) for a in range(size)])


def after(value, results):
    return lax.optimization_barrier((value, *results))[0] if results else value


def ordered(value, axis, strides):
    position = lax.axis_index(axis)
    for stride in strides:
        other = swap(value, axis, stride)
        high = (position // stride) % 2 == 1
        value = jnp.concatenate([jnp.where(high, other, value), jnp.where(high, value, other)], 0)
    return value


def contract(a, b, a_dim, b_dim):
    return lax.dot_general(a, b, (((a_dim,), (b_dim,)), ((), ())), preferred_element_type=jnp.float32)


AHEAD = 3


def products_kernel(count, resume, finish, blocks, scale, starts_ref, mix_ref, right_ref, rows_hbm, *refs):
    pieces = refs[:count]
    refs = refs[count:]
    if resume:
        partial_hbm, refs = refs[0], refs[1:]
    if finish:
        right_out, left_out, loss_out, total, rows_buf, piece_buf, sems = refs
    else:
        total, rows_buf, piece_buf, sems = refs
    slots, _, depth = rows_buf.shape

    def start_of(slot):
        return pl.multiple_of(starts_ref[slot] * depth, depth)

    def copies(slot):
        found = [pltpu.make_async_copy(rows_hbm.at[:, pl.ds(start_of(slot), depth)], rows_buf.at[slot], sems.at[2 * slot])]
        if slot < count:
            found.append(pltpu.make_async_copy(pieces[slot], piece_buf.at[slot], sems.at[2 * slot + 1]))
        return found

    def begin(slot):
        if slot < slots:
            for copy in copies(slot):
                copy.start()

    def await_slot(slot):
        for copy in copies(slot):
            copy.wait()

    if resume:
        fetch = pltpu.make_async_copy(partial_hbm, total, sems.at[2 * slots])
        fetch.start()
    for slot in range(AHEAD):
        begin(slot)
    if resume:
        fetch.wait()
    else:
        total[...] = contract(mix_ref[...], right_ref[...], 1, 0)
    for slot in range(count):
        begin(slot + AHEAD)
        await_slot(slot)
        total[...] -= contract(rows_buf[slot], piece_buf[slot], 1, 0)
    if not finish:
        return

    columns = right_ref.shape[1]
    mids = right_ref.shape[0] // blocks
    in_size = left_out.shape[1] // mids
    residual = total[...]
    loss_out[...] = jnp.sum(residual * residual, axis=0, keepdims=True)
    slope = (residual * scale).astype(jnp.bfloat16)
    full_right = contract(mix_ref[...], slope, 0, 0)
    column_block = lax.broadcasted_iota(jnp.int32, (1, columns), 1) // (columns // blocks)
    grad_right = full_right[:mids]
    for b in range(1, blocks):
        grad_right = jnp.where(column_block == b, full_right[b * mids : (b + 1) * mids], grad_right)
    right_out[...] = grad_right
    back_mix = contract(slope, right_ref[...], 1, 1).T.astype(jnp.bfloat16)
    mid = lax.broadcasted_iota(jnp.int32, (mids, 1), 0)
    lane = lax.broadcasted_iota(jnp.int32, (1, depth), 1)
    for slot in range(slots):
        if slot >= count:
            begin(slot + AHEAD)
            await_slot(slot)
        full_left = contract(back_mix, rows_buf[slot], 1, 0)
        same = mid == (lane + start_of(slot)) // in_size
        sums = [
            jnp.sum(jnp.where(same, full_left[b * mids : (b + 1) * mids], 0.0), axis=0, keepdims=True)
            for b in range(blocks)
        ]
        left_out[:, pl.ds(start_of(slot), depth)] = jnp.concatenate(sums, 0)


def products(rows, mix, right_diag, pieces, starts, blocks, scale, partial=None, finish=True):
    count = len(pieces)
    tokens, features = rows.shape
    mid_columns, columns = right_diag.shape
    depth = pieces[0].shape[0]
    slots = starts.shape[0]
    vmem = pl.BlockSpec(memory_space=pltpu.VMEM)
    far_away = pl.BlockSpec(memory_space=pl.ANY)
    operands = [starts, mix, right_diag, rows, *pieces]
    if partial is not None:
        operands.append(partial)
    in_specs = [pl.BlockSpec(memory_space=pltpu.SMEM), vmem, vmem] + [far_away] * (len(operands) - 3)
    scratch = [
        pltpu.VMEM((slots, tokens, depth), jnp.bfloat16),
        pltpu.VMEM((count, depth, columns), jnp.bfloat16),
        pltpu.SemaphoreType.DMA((2 * slots + 1,)),
    ]
    flops = 2 * tokens * columns * depth * count
    if finish:
        shapes = [(mid_columns // blocks, columns), (blocks, features), (1, columns)]
        scratch = [pltpu.VMEM((tokens, columns), jnp.float32)] + scratch
        flops += 4 * tokens * columns * mid_columns + 2 * tokens * mid_columns * features
    else:
        shapes = [(tokens, columns)]
    results = pl.pallas_call(
        functools.partial(products_kernel, count, partial is not None, finish, blocks, scale),
        out_shape=[jax.ShapeDtypeStruct(shape, jnp.float32) for shape in shapes],
        in_specs=in_specs,
        out_specs=[vmem] * len(shapes),
        scratch_shapes=scratch,
        compiler_params=pltpu.CompilerParams(vmem_limit_bytes=VMEM_BYTES),
        cost_estimate=pl.CostEstimate(
            flops=flops, bytes_accessed=2 * depth * (tokens * slots + columns * count), transcendentals=0
        ),
    )(*operands)
    return results if finish else results[0]


def local(tokens, dense_weight, left_factor, right_factor):
    tok_rows, features = tokens.shape
    weight_rows, columns = dense_weight.shape
    dp_count = lax.axis_size("dp")
    tensor_count = lax.axis_size("tensor")
    dp_pos = lax.axis_index("dp")
    tensor_pos = lax.axis_index("tensor")
    in_size = left_factor.shape[0]
    mids = right_factor.shape[0]
    blocks = left_factor.shape[1] * tensor_count // mids
    own_blocks = blocks // tensor_count
    out_size = columns // own_blocks
    total_tokens = tok_rows * dp_count

    bits = dp_count.bit_length() - 1
    strides = [1 << b for b in range(bits)]
    grouped = max(bits - 3, 0)
    pair = strides[grouped:][len(strides[grouped:]) // 2]
    others = [s for s in reversed(strides[grouped:]) if s != pair]
    pair_bit = (dp_pos // pair) % 2
    unit_rows = weight_rows << grouped

    half_blocks = own_blocks // 2
    chunks = 2 if half_blocks % 2 == 0 else 1
    chunk_blocks = half_blocks // chunks
    chunk_columns = chunk_blocks * out_size
    half_columns = half_blocks * out_size

    def weight_piece(half, chunk):
        start = half * half_columns + chunk * chunk_columns
        return lax.dynamic_slice_in_dim(dense_weight, start, chunk_columns, 1)

    held = [{} for _ in range(chunks)]
    theirs = []
    for chunk in range(chunks):
        held[chunk][0] = ordered(weight_piece(pair_bit, chunk), "dp", strides[:grouped])
        theirs.append(ordered(weight_piece(1 - pair_bit, chunk), "dp", strides[:grouped]))
    far, near = others

    def send(chunk, mask, stride, waits=()):
        held[chunk][mask ^ stride] = swap(after(held[chunk][mask], waits), "dp", stride)
        return held[chunk][mask ^ stride]

    def send_pair(chunk, waits=()):
        held[chunk][pair] = swap(after(theirs[chunk], waits), "dp", pair)
        return held[chunk][pair]

    share = tok_rows // tensor_count
    first_cut = share * 7 // 15 // 16 * 16
    cuts = [0, first_cut, first_cut + (share - first_cut) // 2 // 16 * 16, share]

    def fetch_tokens(which, waits=()):
        begin, size = cuts[which], cuts[which + 1] - cuts[which]
        part = lax.dynamic_slice_in_dim(tokens, tensor_pos * share + begin, size, 0)
        return swap(after(part, waits), "dp", pair)

    def share_tokens(part):
        stride = tensor_count // 2
        while stride:
            part = jnp.concatenate([part, swap(part, "tensor", stride)], 0)
            stride //= 2
        return part

    last = chunks - 1
    parts = [None] * 3
    done = [send(0, 0, far), send_pair(0), send(0, 0, near)]
    if last:
        done.append(send(last, 0, near))
    done = [send(0, pair, far, done), send(0, pair, near, done), send(0, far, near, done)] + (
        [send_pair(last, done)] if last else []
    )
    parts[0] = fetch_tokens(0, done)
    done = [parts[0], send(0, far ^ pair, near, done)] + (
        [send(last, 0, far, done), send(last, pair, near, done)] if last else []
    )
    early_done = done

    left_blocks = left_factor.reshape(in_size, mids // tensor_count, blocks)
    left_blocks = lax.all_to_all(left_blocks, "tensor", split_axis=2, concat_axis=1, tiled=True)
    left_blocks = lax.dynamic_slice_in_dim(left_blocks, pair_bit * half_blocks, half_blocks, 2)
    eye_left = jnp.eye(mids, dtype=jnp.bfloat16)
    left_rows = left_blocks.transpose(1, 0, 2)
    left_diag = (left_rows[:, :, :, None] * eye_left[:, None, None, :]).reshape(features, half_blocks * mids)
    right_half = lax.dynamic_slice_in_dim(right_factor, pair_bit * half_columns, half_columns, 1)

    row_block = jnp.arange(chunk_blocks * mids) // mids
    column_block = jnp.arange(chunk_columns) // out_size
    same_block = row_block[:, None] == column_block[None, :]

    token_sets = [tokens]
    order = [0, near, pair, far, far ^ near, pair ^ near, far ^ pair, far ^ pair ^ near]
    starts = jnp.stack([(dp_pos ^ mask) >> grouped for mask in order]).astype(jnp.int32)
    right_diags = []
    for chunk in range(chunks):
        right_chunk = right_half[:, chunk * chunk_columns : (chunk + 1) * chunk_columns]
        right_diags.append(jnp.where(same_block, jnp.tile(right_chunk, (chunk_blocks, 1)), jnp.bfloat16(0)))
    mixes = {}
    partials = {}
    sums = [None] * chunks
    previous = None

    def run(which, chunk, begin=0, end=len(order), waits=()):
        nonlocal previous
        rows = token_sets[which]
        if which not in mixes:
            mixes[which] = jnp.dot(rows, left_diag, preferred_element_type=jnp.float32).astype(jnp.bfloat16)
        mix = mixes[which][:, chunk * chunk_blocks * mids : (chunk + 1) * chunk_blocks * mids]
        mix = after(mix, [*waits, *([] if previous is None else [previous])])
        pieces = [held[chunk][mask] for mask in order[begin:end]]
        finish = end == len(order)
        places = jnp.concatenate([starts[begin:], starts[:begin]]) if finish else starts[begin:end]
        terms = products(
            rows, mix, right_diags[chunk], pieces, places, chunk_blocks, 1.0 / total_tokens,
            partial=partials[which, chunk] if begin else None, finish=finish,
        )
        if not finish:
            previous = partials[which, chunk] = terms
            return
        previous = terms[2]
        sums[chunk] = terms if sums[chunk] is None else [a + b for a, b in zip(sums[chunk], terms)]

    if last:
        run(0, 0, 0, 6)
        parts[1] = fetch_tokens(1, [previous, *early_done])
        send(last, pair, far, early_done)
        send(last, far, near, early_done)
        parts[2] = fetch_tokens(2, [parts[1]])
        token_sets += [share_tokens(parts[0]), share_tokens(parts[1])]
        run(0, 0, 6, waits=[parts[1]])
        run(0, last, 0, 4)
        run(1, 0)
        send(last, far ^ pair, near, [previous])
        token_sets.append(share_tokens(after(parts[2], [previous])))
        run(1, last, 0, 6)
        run(2, 0)
        run(2, last, 0, 6)
        run(0, last, 4)
        run(1, last, 6)
        run(2, last, 6)
        run(3, 0)
        run(3, last)
    else:
        token_sets += [share_tokens(fetch_tokens(which, early_done)) for which in range(3)]
        for which in range(4):
            run(which, 0)
    loss_part = sum(jnp.sum(terms[2]) for terms in sums)
    right_parts = [terms[0] for terms in sums]
    left_parts = [terms[1] for terms in sums]

    left_sum = jnp.concatenate(left_parts, 0).reshape(half_blocks, mids, in_size).transpose(2, 0, 1)
    both = jnp.concatenate([*right_parts, left_sum.reshape(in_size, half_blocks * mids)], 1)
    width = both.shape[1]
    both = both.reshape((2,) * bits + (both.shape[0] // dp_count, width))
    order = [s for s in reversed(strides)]
    for stride in [near, far] + strides[:grouped]:
        at = order.index(stride)
        bit = (dp_pos // stride) % 2
        away = lax.dynamic_index_in_dim(both, 1 - bit, at, keepdims=False)
        kept = lax.dynamic_index_in_dim(both, bit, at, keepdims=False)
        both = kept + swap(away, "dp", stride)
        order.remove(stride)

    squares = both * both
    scalars = jnp.stack([jnp.sum(squares[..., half_columns:]), jnp.sum(squares[..., :half_columns]), loss_part])
    devices = dp_count * tensor_count
    scalars = jnp.broadcast_to(scalars[None], (devices, 3))
    sq_left, sq_right, loss_all = jnp.sum(lax.all_to_all(scalars, ("dp", "tensor"), 0, 0, tiled=True), 0)

    right_both = both[..., :half_columns]
    away = lax.dynamic_index_in_dim(right_both, 1 - pair_bit, 0, keepdims=False)
    kept = lax.dynamic_index_in_dim(right_both, pair_bit, 0, keepdims=False)
    other = swap(away, "dp", pair)
    right_rows = jnp.concatenate([jnp.where(pair_bit == 0, kept, other), jnp.where(pair_bit == 0, other, kept)], 1)

    left_both = both[..., half_columns:].reshape(2, -1, half_blocks, tensor_count, mids // tensor_count)
    left_both = left_both.transpose(0, 3, 1, 4, 2)
    groups = []
    for base in range(dp_count):
        if not base & pair:
            groups.append([d * tensor_count + t for d in (base, base | pair) for t in range(tensor_count)])
    left_both = left_both.reshape((2 * tensor_count,) + left_both.shape[2:])
    left_both = lax.all_to_all(left_both, ("dp", "tensor"), 0, 0, axis_index_groups=groups, tiled=True)
    left_both = left_both.reshape((2, tensor_count) + left_both.shape[1:])
    left_rows = left_both.transpose(2, 3, 1, 0, 4)
    left_rows = left_rows.reshape(left_rows.shape[0], -1)
    dir_left = left_rows * lax.rsqrt(sq_left / (features * blocks) + epsilon)
    dir_right = right_rows * lax.rsqrt(sq_right / (mids * columns * tensor_count) + epsilon)
    loss = loss_all / (2.0 * total_tokens)
    return (dir_left, dir_right, loss)


def solution(mesh):
    in_specs = (P("dp", None), P("dp", "tensor"), P(None, "tensor"), P(None, "tensor"))
    out_specs = (P("dp", "tensor"), P("dp", "tensor"), P())
    return jax.shard_map(local, mesh=mesh, in_specs=in_specs, out_specs=out_specs, check_vma=False)
```

time: 549 us -> 359 us (0.65)
  matrix products: 201 us -> 13.2 us
  Pallas kernels: 0 us -> 113 us
  waiting for transfers between devices: 207 us -> 114 us
  blocking collectives: 39.2 us -> 0 us
  starting transfers between devices: 29.8 us -> 40.6 us
  local copies, waits for them, and re-layouts: 36.7 us -> 44.4 us
    dot_general x46 -> x4, matrix products: 201 us -> 13.2 us  [run(): jnp.dot(rows, left_diag, preferred_element_type=jnp.float32)]
    pallas_call x0 -> x12, Pallas kernels: none -> 113 us  [products(): pl.pallas_call(functools.partial(products_kernel, count, partial is not N...]
    ppermute x20 -> x26, waiting for transfers between devices: 205 us -> 108 us  [swap(): return lax.ppermute(value, axis, [(a, a ^ stride) for a in range(size)])]
    psum x1 -> x0, blocking collectives: 39.2 us -> none  [local(): lax.psum((jnp.sum(left_rows * left_rows), jnp.sum(right_rows * right_rows...]
    ppermute x20 -> x26, starting transfers between devices: 22.7 us -> 30.2 us  [swap(): return lax.ppermute(value, axis, [(a, a ^ stride) for a in range(size)])]
    select_n x4 -> x1, other arithmetic: 6.26 us -> 0.01 us  [local(): jnp.where(pair_bit == 0, kept, other)]
    unnamed x89 -> x92, local copies, waits for them, and re-layouts: 7.62 us -> 11 us
  transfers between devices with their start and end apart: 22 -> 29, of which waited for: 11 -> 13; matrix products, arithmetic and copies ran while one was open for 25% -> 18% of each run, Pallas kernels for 0% -> 27%
where the time goes in v3:
time: 359 us; the launch traced here: 354 us
  waiting for transfers between devices  114 us (32%)
  Pallas kernels  113 us (31%)
  local copies, waits for them, and re-layouts  44.4 us (12%)
  starting transfers between devices  40.6 us (11%)
  other arithmetic  21.3 us (6%)
  matrix products  13.2 us (4%)
  between operations  6.6 us (2%)
    pallas_call x12, Pallas kernels, products(): pl.pallas_call(functools.partial(products_kernel, count, partial is not N...  113 us
    ppermute x26, waiting for transfers between devices, swap(): return lax.ppermute(value, axis, [(a, a ^ stride) for a in range(size)])  108 us
    ppermute x26, starting transfers between devices, swap(): return lax.ppermute(value, axis, [(a, a ^ stride) for a in range(size)])  30.2 us
    dot_general x4, matrix products, run(): jnp.dot(rows, left_diag, preferred_element_type=jnp.float32)  13.2 us
    mul x1, local copies, waits for them, and re-layouts, local(): left_rows[:, :, :, None] * eye_left[:, None, None, :]  12 us
    unnamed x92, local copies, waits for them, and re-layouts  11 us
    mul x1, other arithmetic, local(): left_rows[:, :, :, None] * eye_left[:, None, None, :]  8.59 us
  transfers between devices with their start and end apart: 29, of which 13 were waited for; matrix products, arithmetic and copies ran while one was open for 18% of the time, Pallas kernels for 27%

profile of v3, /device:TPU:0, one launch (start us, length us, event | category | flops | bytes accessed | tf_op | source)
XLA Modules:
  0.0 353.8 jit_solution(16753893727101035058)
XLA Ops:
  0.7 3.6 %constant_dynamic-slice_fusion.2 = (bf16[512,896]{1,0:T(8,128)(2,1)}, bf16[512,896]{1,0:T(8,128)(2,1)}, bf16[512,896]{1,0:T(8,128)(2,1)S(1)}, bf16[512,896]{1,0:T(8,128)(2,1)S(1)}) fusion(bf16[512,3584]{1,0:T(8,128)(2,1)} %param.5, s32[]{:T(128)S(6)} %select_n.121, s32[]{:T(128)S(6)} %select_n.118, s32[]{:T(128)S(6)} %select_n.116, s32[]{:T(128)S(6)} %select_n.119), kind=kLoop, calls=%fused_computation.48 | loop fusion | bytes 7340048 | tf_op jit(solution)/shard_map/dynamic_slice | solution.py:180
  4.3 2.9 collective-permute-start
  7.3 2.6 collective-permute-start.2
  11.3 3.3 all-to-all-start
  14.7 1.6 collective-permute-start.1
  16.9 2.2 constant_dynamic-slice_fusion.3
  20.0 1.2 compare_select_fusion
  21.8 2.3 constant_dynamic-slice_fusion.8
  24.5 1.3 copy.51
  25.8 2.7 collective-permute-done.refs_1_
  28.5 27.7 %collective-permute-done.1.refs_2_ = bf16[512,896]{1,0:T(8,128)(2,1)} collective-permute-done((bf16[512,896]{1,0:T(8,128)(2,1)}, bf16[512,896]{1,0:T(8,128)(2,1)}, u32[]{:S(2)}, u32[]{:S(2)}) %collective-permute-start.1) | collective-permute-done | bytes 917536 | tf_op jit(solution)/shard_map/ppermute | solution.py:16
  57.3 1.5 collective-permute-start.4
  58.8 2.5 collective-permute-start.7
  61.3 8.6 %broadcast_multiply_fusion = bf16[64,64,8,64]{3,2,1,0:T(8,128)(2,1)} fusion(bf16[64,64]{1,0:T(8,128)(2,1)S(1)} %fusion.1, bf16[64,64,8]{2,1,0:T(8,128)(2,1)} %copy.51), kind=kLoop, calls=%fused_computation | loop fusion | flops 2097152 | bytes 4268032 | tf_op jit(solution)/shard_map/mul | solution.py:232
  69.9 12.0 %mul.62 = bf16[4096,512]{1,0:T(8,128)(2,1)} reshape(bf16[64,64,8,64]{3,2,1,0:T(8,128)(2,1)} %broadcast_multiply_fusion) | data formatting | bytes 8388608 | tf_op jit(solution)/shard_map/mul | solution.py:232
  81.9 16.3 %collective-permute-done.4.refs_4_ = bf16[512,896]{1,0:T(8,128)(2,1)} collective-permute-done((bf16[512,896]{1,0:T(8,128)(2,1)}, bf16[512,896]{1,0:T(8,128)(2,1)}, u32[]{:S(2)}, u32[]{:S(2)}) %collective-permute-start.4) | collective-permute-done | bytes 917536 | tf_op jit(solution)/shard_map/ppermute | solution.py:16
  98.2 1.0 collective-permute-done.6.refs_0_.refs_6_
  99.2 1.2 collective-permute-done.7.refs_2_
  101.0 2.0 collective-permute-start.10
  103.1 1.5 collective-permute-start.11
  104.5 8.6 %fusion = bf16[960,512]{1,0:T(8,128)(2,1)S(1)} fusion(bf16[960,4096]{1,0:T(8,128)(2,1)} %rows_hbm.7, bf16[4096,512]{1,0:T(8,128)(2,1)} %mul.62), kind=kOutput, calls=%fused_computation.3 | convolution fusion | flops 4027023360 | bytes 13041664 | tf_op jit(solution)/shard_map/dot_general | solution.py:255
  113.2 1.0 fusion.6
  114.2 11.7 %shard_map.67.refs_2_ = f32[960,896]{1,0:T(8,128)} custom-call(s32[6]{0:T(128)} %stack.51.starts_ref, bf16[960,256]{1,0:T(8,128)(2,1)} %get-tuple-element.59.mix_ref, bf16[256,896]{1,0:T(8,128)(2,1)} %get-tuple-element.120.right_ref, bf16[960,4096]{1,0:T(8,128)(2,1)} %rows_hbm.7, bf16[512,896]{1,0:T(8,128)(2,1)} %copy-done.8, ...), custom_call_target="tpu_custom_call" | custom-call | flops 5284823040 | bytes 11403264 | tf_op jit(solution)/shard_map/pallas_call | solution.py:136
  125.9 13.4 %collective-permute-done.8 = bf16[112,4096]{1,0:T(8,128)(2,1)S(1)} collective-permute-done((bf16[112,4096]{1,0:T(8,128)(2,1)}, bf16[112,4096]{1,0:T(8,128)(2,1)S(1)}, u32[]{:S(2)}, u32[]{:S(2)}) %collective-permute-start.8) | collective-permute-done | bytes 917536 | tf_op jit(solution)/shard_map/ppermute | solution.py:16
  139.3 4.1 %collective-permute-done.10.refs_3_ = bf16[512,896]{1,0:T(8,128)(2,1)S(1)} collective-permute-done((bf16[512,896]{1,0:T(8,128)(2,1)S(1)}, bf16[512,896]{1,0:T(8,128)(2,1)S(1)}, u32[]{:S(2)}, u32[]{:S(2)}) %collective-permute-start.10) | collective-permute-done | bytes 917536 | tf_op jit(solution)/shard_map/ppermute | solution.py:16
  146.8 1.2 collective-permute-start.17
  148.0 1.5 collective-permute-start.21
  149.5 1.3 collective-permute-start.13
  150.8 2.2 constant_dynamic-update-slice_fusion.2
  153.1 10.1 %collective-permute-done.12 = bf16[64,4096]{1,0:T(8,128)(2,1)} collective-permute-done((bf16[64,4096]{1,0:T(8,128)(2,1)S(1)}, bf16[64,4096]{1,0:T(8,128)(2,1)}, u32[]{:S(2)}, u32[]{:S(2)}) %collective-permute-start.12) | collective-permute-done | bytes 524320 | tf_op jit(solution)/shard_map/ppermute | solution.py:16
  163.2 12.7 %shard_map.68 = (f32[64,896]{1,0:T(8,128)}, f32[4,4096]{1,0:T(4,128)}, f32[1,896]{1,0:T(1,128)}) custom-call(s32[8]{0:T(128)} %concatenate.52.starts_ref, bf16[960,256]{1,0:T(8,128)(2,1)} %get-tuple-element.59.mix_ref, bf16[256,896]{1,0:T(8,128)(2,1)} %get-tuple-element.120.right_ref, bf16[960,4096]{1,0:T(8,128)(2,1)} %rows_hbm.7, ...), custom_call_target="tpu_custom_call" | custom-call | flops 4655677440 | bytes 9699328 | tf_op jit(solution)/shard_map/pallas_call | solution.py:136
  175.9 1.4 collective-permute-start.15
  177.3 9.2 %shard_map.69.refs_4_ = f32[960,896]{1,0:T(8,128)} custom-call(s32[4]{0:T(128)} %pad_add_fusion.starts_ref, bf16[960,256]{1,0:T(8,128)(2,1)} %get-tuple-element.74.mix_ref, bf16[256,896]{1,0:T(8,128)(2,1)} %get-tuple-element.119.right_ref, bf16[960,4096]{1,0:T(8,128)(2,1)} %rows_hbm.7, bf16[512,896]{1,0:T(8,128)(2,1)} %copy-done, ...), custom_call_target="tpu_custom_call" | custom-call | flops 3523215360 | bytes 7602176 | tf_op jit(solution)/shard_map/pallas_call | solution.py:136
  186.6 1.2 constant_dynamic-update-slice_fusion.5
  187.8 1.3 pad_maximum_fusion.1
  189.2 1.7 pad_maximum_fusion
  191.3 1.2 constant_dynamic-update-slice_fusion.1
  192.6 1.1 constant_dynamic-update-slice_fusion.4
  193.8 1.2 convolution_convert_fusion.3
  196.0 2.1 convolution_convert_fusion.1
  198.9 10.9 %shard_map.70 = (f32[64,896]{1,0:T(8,128)}, f32[4,4096]{1,0:T(4,128)}, f32[1,896]{1,0:T(1,128)}) custom-call(s32[8]{0:T(128)} %stack.52.starts_ref, bf16[448,256]{1,0:T(8,128)(2,1)} %get-tuple-element.63.mix_ref, bf16[256,896]{1,0:T(8,128)(2,1)} %get-tuple-element.120.right_ref, bf16[448,4096]{1,0:T(8,128)(2,1)} %copy-done.10, bf16[512,896]{1,0:T(8,128)(2,1)} %copy-done.8, ...), custom_call_target="tpu_custom_call" | custom-call | flops 4638900224 | bytes 11010048 | tf_op jit(solution)/shard_map/pallas_call | solution.py:136
  209.8 1.4 collective-permute-start.19
  211.2 1.0 copy-done.7
  212.2 7.6 %shard_map.71.refs_2_ = f32[448,896]{1,0:T(8,128)} custom-call(s32[6]{0:T(128)} %stack.51.starts_ref, bf16[448,256]{1,0:T(8,128)(2,1)} %get-tuple-element.78.mix_ref, bf16[256,896]{1,0:T(8,128)(2,1)} %get-tuple-element.119.right_ref, bf16[448,4096]{1,0:T(8,128)(2,1)} %copy-done.10, bf16[512,896]{1,0:T(8,128)(2,1)} %copy-done, bf16[512,896]{1,0:T(8,128)(2,1)} %copy-done.2, ...), custom_call_target="tpu_custom_call" | custom-call | flops 2466250752 | bytes 8257536 | tf_op jit(solution)/shard_map/pallas_call | solution.py:136
  219.8 8.2 %shard_map.72 = (f32[64,896]{1,0:T(8,128)}, f32[4,4096]{1,0:T(4,128)}, f32[1,896]{1,0:T(1,128)}) custom-call(s32[8]{0:T(128)} %stack.52.starts_ref, bf16[256,256]{1,0:T(8,128)(2,1)} %get-tuple-element.68.mix_ref, bf16[256,896]{1,0:T(8,128)(2,1)} %get-tuple-element.120.right_ref, bf16[256,4096]{1,0:T(8,128)(2,1)} %copy-done.1, bf16[512,896]{1,0:T(8,128)(2,1)} %copy-done.8, ...), custom_call_target="tpu_custom_call" | custom-call | flops 2650800128 | bytes 9437184 | tf_op jit(solution)/shard_map/pallas_call | solution.py:136
  228.1 6.1 %shard_map.73.refs_2_ = f32[256,896]{1,0:T(8,128)} custom-call(s32[6]{0:T(128)} %stack.51.starts_ref, bf16[256,256]{1,0:T(8,128)(2,1)} %get-tuple-element.80.mix_ref, bf16[256,896]{1,0:T(8,128)(2,1)} %get-tuple-element.119.right_ref, bf16[256,4096]{1,0:T(8,128)(2,1)} %copy-done.1, bf16[512,896]{1,0:T(8,128)(2,1)} %copy-done, bf16[512,896]{1,0:T(8,128)(2,1)} %copy-done.2, ...), custom_call_target="tpu_custom_call" | custom-call | flops 1409286144 | bytes 7077888 | tf_op jit(solution)/shard_map/pallas_call | solution.py:136
  234.3 1.2 pad_maximum_fusion.2
  235.6 20.8 %collective-permute-done.22.refs_3_.refs_1_.refs_7_ = bf16[512,896]{1,0:T(8,128)(2,1)S(1)} collective-permute-done((bf16[512,896]{1,0:T(8,128)(2,1)S(1)}, bf16[512,896]{1,0:T(8,128)(2,1)S(1)}, u32[]{:S(2)}, u32[]{:S(2)}) %collective-permute-start.22) | collective-permute-done | bytes 917536 | tf_op jit(solution)/shard_map/ppermute | solution.py:16
  257.3 14.5 %shard_map.74 = (f32[64,896]{1,0:T(8,128)}, f32[4,4096]{1,0:T(4,128)}, f32[1,896]{1,0:T(1,128)}) custom-call(s32[8]{0:T(128)} %concatenate.59.starts_ref, bf16[960,256]{1,0:T(8,128)(2,1)} %get-tuple-element.74.mix_ref, bf16[256,896]{1,0:T(8,128)(2,1)} %get-tuple-element.119.right_ref, bf16[960,4096]{1,0:T(8,128)(2,1)} %rows_hbm.7, ...), custom_call_target="tpu_custom_call" | custom-call | flops 6417285120 | bytes 11534336 | tf_op jit(solution)/shard_map/pallas_call | solution.py:136
  271.8 8.4 %shard_map.75 = (f32[64,896]{1,0:T(8,128)}, f32[4,4096]{1,0:T(4,128)}, f32[1,896]{1,0:T(1,128)}) custom-call(s32[8]{0:T(128)} %concatenate.52.starts_ref, bf16[448,256]{1,0:T(8,128)(2,1)} %get-tuple-element.78.mix_ref, bf16[256,896]{1,0:T(8,128)(2,1)} %get-tuple-element.119.right_ref, bf16[448,4096]{1,0:T(8,128)(2,1)} %copy-done.10, ...), custom_call_target="tpu_custom_call" | custom-call | flops 2172649472 | bytes 5505024 | tf_op jit(solution)/shard_map/pallas_call | solution.py:136
  280.3 7.1 %shard_map.76 = (f32[64,896]{1,0:T(8,128)}, f32[4,4096]{1,0:T(4,128)}, f32[1,896]{1,0:T(1,128)}) custom-call(s32[8]{0:T(128)} %concatenate.52.starts_ref, bf16[256,256]{1,0:T(8,128)(2,1)} %get-tuple-element.80.mix_ref, bf16[256,896]{1,0:T(8,128)(2,1)} %get-tuple-element.119.right_ref, bf16[256,4096]{1,0:T(8,128)(2,1)} %copy-done.1, ...), custom_call_target="tpu_custom_call" | custom-call | flops 1241513984 | bytes 3932160 | tf_op jit(solution)/shard_map/pallas_call | solution.py:136
  287.5 1.2 convolution_convert_fusion.2
  289.5 8.4 %shard_map.77 = (f32[64,896]{1,0:T(8,128)}, f32[4,4096]{1,0:T(4,128)}, f32[1,896]{1,0:T(1,128)}) custom-call(s32[8]{0:T(128)} %stack.52.starts_ref, bf16[256,256]{1,0:T(8,128)(2,1)} %get-tuple-element.82.mix_ref, bf16[256,896]{1,0:T(8,128)(2,1)} %get-tuple-element.120.right_ref, bf16[256,4096]{1,0:T(8,128)(2,1)} %copy-done.5, bf16[512,896]{1,0:T(8,128)(2,1)} %copy-done.8, ...), custom_call_target="tpu_custom_call" | custom-call | flops 2650800128 | bytes 9437184 | tf_op jit(solution)/shard_map/pallas_call | solution.py:136
  298.1 8.4 %shard_map.78 = (f32[64,896]{1,0:T(8,128)}, f32[4,4096]{1,0:T(4,128)}, f32[1,896]{1,0:T(1,128)}) custom-call(s32[8]{0:T(128)} %stack.52.starts_ref, bf16[256,256]{1,0:T(8,128)(2,1)} %get-tuple-element.88.mix_ref, bf16[256,896]{1,0:T(8,128)(2,1)} %get-tuple-element.119.right_ref, bf16[256,4096]{1,0:T(8,128)(2,1)} %copy-done.5, bf16[512,896]{1,0:T(8,128)(2,1)} %copy-done, ...), custom_call_target="tpu_custom_call" | custom-call | flops 2650800128 | bytes 9437184 | tf_op jit(solution)/shard_map/pallas_call | solution.py:136
  309.5 7.6 %collective-permute-done.23 = f32[2,2,8,2304]{3,2,1,0:T(8,128)S(1)} collective-permute-done((f32[2,2,8,2304]{3,2,1,0:T(8,128)S(1)}, f32[2,2,8,2304]{3,2,1,0:T(8,128)S(1)}, u32[]{:S(2)}, u32[]{:S(2)}) %collective-permute-start.23) | collective-permute-done | bytes 294944 | tf_op jit(solution)/shard_map/ppermute | solution.py:16
  317.2 3.9 %collective-permute-start.24 = (f32[2,8,2304]{2,1,0:T(8,128)S(1)}, f32[2,8,2304]{2,1,0:T(8,128)S(1)}, u32[]{:S(2)}, u32[]{:S(2)}) collective-permute-start(f32[2,8,2304]{2,1,0:T(8,128)S(1)} %dynamic-slice_bitcast_fusion.1), channel_id=1, source_target_pairs={{0,16},{4,20},{8,24},{12,28},{16,0},{20,4},{24,8},{28,12},{1,17},{... | collective-permute-start | bytes 442376 | tf_op jit(solution)/shard_map/ppermute | solution.py:16
  323.1 3.2 collective-permute-done.24
  327.6 1.4 pad_maximum_fusion.5
  329.6 3.7 %all-to-all-start.2 = ((f32[32,1,3]{2,1,0:T(1,128)}), f32[32,1,3]{2,1,0:T(1,128)S(1)}, u32[]{:S(2)}, u32[]{:S(2)}) async-start(f32[32,1,3]{2,1,0:T(1,128)} %broadcast_in_dim.8), calls=%async_computation.2 | async-start | bytes 32768 | tf_op jit(solution)/shard_map/all_to_all | solution.py:316
  334.4 1.8 collective-permute-start.25
  336.1 4.2 %all-to-all-done.2 = f32[32,1,3]{2,1,0:T(1,128)S(1)} async-done(((f32[32,1,3]{2,1,0:T(1,128)}), f32[32,1,3]{2,1,0:T(1,128)S(1)}, u32[]{:S(2)}, u32[]{:S(2)}) %all-to-all-start.2) | async-done | bytes 416 | tf_op jit(solution)/shard_map/all_to_all | solution.py:316
  340.4 3.3 all-to-all-start.1
  346.5 1.9 all-to-all-done.1
  350.2 1.4 mul.71
  (163 shorter events, 22.9 us)
Async XLA Ops:
  0.7 9.2 %copy-start.25 = (bf16[64,1024]{1,0:T(8,128)(2,1)S(1)}, bf16[64,1024]{1,0:T(8,128)(2,1)}, u32[]{:S(2)}) copy-start(bf16[64,1024]{1,0:T(8,128)(2,1)} %param.6) | copy-start | bytes 393220
  4.3 20.0 %copy-start.8 = (bf16[512,896]{1,0:T(8,128)(2,1)}, bf16[512,896]{1,0:T(8,128)(2,1)S(1)}, u32[]{:S(2)}) copy-start(bf16[512,896]{1,0:T(8,128)(2,1)S(1)} %get-tuple-element.105.refs_0_) | copy-start | bytes 2752516
  4.3 96.7 %copy-start = (bf16[512,896]{1,0:T(8,128)(2,1)}, bf16[512,896]{1,0:T(8,128)(2,1)S(1)}, u32[]{:S(2)}) copy-start(bf16[512,896]{1,0:T(8,128)(2,1)S(1)} %get-tuple-element.56.refs_0_) | copy-start | bytes 2752516
  4.3 24.2 %collective-permute-start = (bf16[512,896]{1,0:T(8,128)(2,1)S(1)}, bf16[512,896]{1,0:T(8,128)(2,1)}, u32[]{:S(2)}, u32[]{:S(2)}) collective-permute-start(bf16[512,896]{1,0:T(8,128)(2,1)S(1)} %get-tuple-element.105.refs_0_), channel_id=1, source_target_pairs={{0,4},{4,0},{8,12},{12,8},{16,20},{20,16},{24,28},{28,24},{1,5},{5... | collective-permute-start | bytes 2752520 | tf_op jit(solution)/shard_map/ppermute | solution.py:16
  7.3 49.0 %collective-permute-start.2 = (bf16[512,896]{1,0:T(8,128)(2,1)S(1)}, bf16[512,896]{1,0:T(8,128)(2,1)}, u32[]{:S(2)}, u32[]{:S(2)}) collective-permute-start(bf16[512,896]{1,0:T(8,128)(2,1)S(1)} %get-tuple-element.105.refs_0_), channel_id=1, source_target_pairs={{0,16},{4,20},{8,24},{12,28},{16,0},{20,4},{24,8},{28,12},{1,17},{... | collective-permute-start | bytes 2752520 | tf_op jit(solution)/shard_map/ppermute | solution.py:16
  11.3 12.8 %all-to-all-start = ((bf16[4,2,8192]{2,1,0:T(2,128)(2,1)}), bf16[4,2,8192]{2,1,0:T(2,128)(2,1)S(1)}, u32[]{:S(2)}, u32[]{:S(2)}) async-start(bf16[4,2,8192]{2,1,0:T(2,128)(2,1)} %reshape.99), calls=%async_computation | async-start | bytes 262144 | tf_op jit(solution)/shard_map/all_to_all | solution.py:228
  14.7 41.6 %collective-permute-start.1 = (bf16[512,896]{1,0:T(8,128)(2,1)}, bf16[512,896]{1,0:T(8,128)(2,1)}, u32[]{:S(2)}, u32[]{:S(2)}) collective-permute-start(bf16[512,896]{1,0:T(8,128)(2,1)} %get-tuple-element.104), channel_id=1, source_target_pairs={{0,8},{4,12},{8,0},{12,4},{16,24},{20,28},{24,16},{28,20},{1,9},{5... | collective-permute-start | bytes 2752520 | tf_op jit(solution)/shard_map/ppermute | solution.py:16
  16.3 40.0 %collective-permute-start.3 = (bf16[512,896]{1,0:T(8,128)(2,1)S(1)}, bf16[512,896]{1,0:T(8,128)(2,1)S(1)}, u32[]{:S(2)}, u32[]{:S(2)}) collective-permute-start(bf16[512,896]{1,0:T(8,128)(2,1)S(1)} %get-tuple-element.56.refs_0_), channel_id=1, source_target_pairs={{0,4},{4,0},{8,12},{12,8},{16,20},{20,16},{24,28},{28,24},{1,5},{5... | collective-permute-start | bytes 2752520 | tf_op jit(solution)/shard_map/ppermute | solution.py:16
  56.3 13.6 %copy-start.2 = (bf16[512,896]{1,0:T(8,128)(2,1)}, bf16[512,896]{1,0:T(8,128)(2,1)S(1)}, u32[]{:S(2)}) copy-start(bf16[512,896]{1,0:T(8,128)(2,1)S(1)} %collective-permute-done.3.refs_1_) | copy-start | bytes 2752516
  56.3 41.9 %collective-permute-start.5 = (bf16[512,896]{1,0:T(8,128)(2,1)}, bf16[512,896]{1,0:T(8,128)(2,1)}, u32[]{:S(2)}, u32[]{:S(2)}) collective-permute-start(bf16[512,896]{1,0:T(8,128)(2,1)} %collective-permute-done.1.refs_2_), channel_id=1, source_target_pairs={{0,4},{4,0},{8,12},{12,8},{16,20},{20,16},{24,28},{28,24},{1,5},{5... | collective-permute-start | bytes 2752520 | tf_op jit(solution)/shard_map/ppermute | solution.py:16
  56.8 42.4 %collective-permute-start.6 = (bf16[512,896]{1,0:T(8,128)(2,1)}, bf16[512,896]{1,0:T(8,128)(2,1)}, u32[]{:S(2)}, u32[]{:S(2)}) collective-permute-start(bf16[512,896]{1,0:T(8,128)(2,1)} %collective-permute-done.1.refs_2_), channel_id=1, source_target_pairs={{0,16},{4,20},{8,24},{12,28},{16,0},{20,4},{24,8},{28,12},{1,17},{... | collective-permute-start | bytes 2752520 | tf_op jit(solution)/shard_map/ppermute | solution.py:16
  57.3 40.9 %collective-permute-start.4 = (bf16[512,896]{1,0:T(8,128)(2,1)}, bf16[512,896]{1,0:T(8,128)(2,1)}, u32[]{:S(2)}, u32[]{:S(2)}) collective-permute-start(bf16[512,896]{1,0:T(8,128)(2,1)} %collective-permute-done.2.refs_3_), channel_id=1, source_target_pairs={{0,4},{4,0},{8,12},{12,8},{16,20},{20,16},{24,28},{28,24},{1,5},{5... | collective-permute-start | bytes 2752520 | tf_op jit(solution)/shard_map/ppermute | solution.py:16
  58.8 41.6 %collective-permute-start.7 = (bf16[512,896]{1,0:T(8,128)(2,1)}, bf16[512,896]{1,0:T(8,128)(2,1)S(1)}, u32[]{:S(2)}, u32[]{:S(2)}) collective-permute-start(bf16[512,896]{1,0:T(8,128)(2,1)} %get-tuple-element.53), channel_id=1, source_target_pairs={{0,8},{4,12},{8,0},{12,4},{16,24},{20,28},{24,16},{28,20},{1,9},{5... | collective-permute-start | bytes 2752520 | tf_op jit(solution)/shard_map/ppermute | solution.py:16
  100.4 47.6 %copy-start.3 = (bf16[512,896]{1,0:T(8,128)(2,1)}, bf16[512,896]{1,0:T(8,128)(2,1)S(1)}, u32[]{:S(2)}) copy-start(bf16[512,896]{1,0:T(8,128)(2,1)S(1)} %collective-permute-done.7.refs_2_) | copy-start | bytes 2752516
  100.4 38.9 %collective-permute-start.8 = (bf16[112,4096]{1,0:T(8,128)(2,1)}, bf16[112,4096]{1,0:T(8,128)(2,1)S(1)}, u32[]{:S(2)}, u32[]{:S(2)}) collective-permute-start(bf16[112,4096]{1,0:T(8,128)(2,1)} %constant_dynamic-slice_fusion.3), channel_id=1, source_target_pairs={{0,8},{4,12},{8,0},{12,4},{16,24},{20,28},{24,16},{28,20},{1,9},{5... | collective-permute-start | bytes 2752520 | tf_op jit(solution)/shard_map/ppermute | solution.py:16
  100.4 38.9 %collective-permute-start.9 = (bf16[512,896]{1,0:T(8,128)(2,1)}, bf16[512,896]{1,0:T(8,128)(2,1)S(1)}, u32[]{:S(2)}, u32[]{:S(2)}) collective-permute-start(bf16[512,896]{1,0:T(8,128)(2,1)} %collective-permute-done.6.refs_0_.refs_6_), channel_id=1, source_target_pairs={{0,4},{4,0},{8,12},{12,8},{16,20},{20,16},{24,28},{28,24},{1,5},{5... | collective-permute-start | bytes 2752520 | tf_op jit(solution)/shard_map/ppermute | solution.py:16
  101.0 42.3 %collective-permute-start.10 = (bf16[512,896]{1,0:T(8,128)(2,1)S(1)}, bf16[512,896]{1,0:T(8,128)(2,1)S(1)}, u32[]{:S(2)}, u32[]{:S(2)}) collective-permute-start(bf16[512,896]{1,0:T(8,128)(2,1)S(1)} %get-tuple-element.56.refs_0_), channel_id=1, source_target_pairs={{0,16},{4,20},{8,24},{12,28},{16,0},{20,4},{24,8},{28,12},{1,17},{... | collective-permute-start | bytes 2752520 | tf_op jit(solution)/shard_map/ppermute | solution.py:16
  103.1 40.3 %collective-permute-start.11 = (bf16[512,896]{1,0:T(8,128)(2,1)S(1)}, bf16[512,896]{1,0:T(8,128)(2,1)S(1)}, u32[]{:S(2)}, u32[]{:S(2)}) collective-permute-start(bf16[512,896]{1,0:T(8,128)(2,1)S(1)} %collective-permute-done.7.refs_2_), channel_id=1, source_target_pairs={{0,4},{4,0},{8,12},{12,8},{16,20},{20,16},{24,28},{28,24},{1,5},{5... | collective-permute-start | bytes 2752520 | tf_op jit(solution)/shard_map/ppermute | solution.py:16
  114.2 30.2 %copy-start.17 = (bf16[64,4096]{1,0:T(8,128)(2,1)S(1)}, bf16[64,4096]{1,0:T(8,128)(2,1)}, u32[]{:S(2)}) copy-start(bf16[64,4096]{1,0:T(8,128)(2,1)} %get-tuple-element.58) | copy-start | bytes 1572868
  139.3 5.1 %copy-start.16 = (bf16[112,4096]{1,0:T(8,128)(2,1)}, bf16[112,4096]{1,0:T(8,128)(2,1)S(1)}, u32[]{:S(2)}) copy-start(bf16[112,4096]{1,0:T(8,128)(2,1)S(1)} %collective-permute-done.8) | copy-start | bytes 2752516
  139.3 5.1 %copy-start.13 = (bf16[512,896]{1,0:T(8,128)(2,1)}, bf16[512,896]{1,0:T(8,128)(2,1)S(1)}, u32[]{:S(2)}) copy-start(bf16[512,896]{1,0:T(8,128)(2,1)S(1)} %collective-permute-done.9.refs_1_.refs_7_) | copy-start | bytes 2752516
  143.4 32.5 %copy-start.4 = (bf16[512,896]{1,0:T(8,128)(2,1)}, bf16[512,896]{1,0:T(8,128)(2,1)S(1)}, u32[]{:S(2)}) copy-start(bf16[512,896]{1,0:T(8,128)(2,1)S(1)} %collective-permute-done.10.refs_3_) | copy-start | bytes 2752516
  144.4 18.8 %collective-permute-start.12 = (bf16[64,4096]{1,0:T(8,128)(2,1)S(1)}, bf16[64,4096]{1,0:T(8,128)(2,1)}, u32[]{:S(2)}, u32[]{:S(2)}) collective-permute-start(bf16[64,4096]{1,0:T(8,128)(2,1)S(1)} %copy-done.17), channel_id=1, source_target_pairs={{0,8},{4,12},{8,0},{12,4},{16,24},{20,28},{24,16},{28,20},{1,9},{5... | collective-permute-start | bytes 1572872 | tf_op jit(solution)/shard_map/ppermute | solution.py:16
  146.8 64.4 %collective-permute-start.17 = (bf16[512,896]{1,0:T(8,128)(2,1)S(1)}, bf16[512,896]{1,0:T(8,128)(2,1)S(1)}, u32[]{:S(2)}, u32[]{:S(2)}) collective-permute-start(bf16[512,896]{1,0:T(8,128)(2,1)S(1)} %collective-permute-done.10.refs_3_), channel_id=1, source_target_pairs={{0,4},{4,0},{8,12},{12,8},{16,20},{20,16},{24,28},{28,24},{1,5},{5... | collective-permute-start | bytes 2752520 | tf_op jit(solution)/shard_map/ppermute | solution.py:16
  148.0 86.2 %collective-permute-start.21 = (bf16[512,896]{1,0:T(8,128)(2,1)S(1)}, bf16[512,896]{1,0:T(8,128)(2,1)S(1)}, u32[]{:S(2)}, u32[]{:S(2)}) collective-permute-start(bf16[512,896]{1,0:T(8,128)(2,1)S(1)} %collective-permute-done.7.refs_2_), channel_id=1, source_target_pairs={{0,16},{4,20},{8,24},{12,28},{16,0},{20,4},{24,8},{28,12},{1,17},{... | collective-permute-start | bytes 2752520 | tf_op jit(solution)/shard_map/ppermute | solution.py:16
  149.5 39.7 %collective-permute-start.13 = (bf16[112,4096]{1,0:T(8,128)(2,1)}, bf16[112,4096]{1,0:T(8,128)(2,1)}, u32[]{:S(2)}, u32[]{:S(2)}) collective-permute-start(bf16[112,4096]{1,0:T(8,128)(2,1)} %copy-done.16), channel_id=1, source_target_pairs={{0,2},{1,3},{2,0},{3,1},{4,6},{5,7},{6,4},{7,5},{8,10},{9,11},{10,... | collective-permute-start | bytes 2752520 | tf_op jit(solution)/shard_map/ppermute | solution.py:16
  163.2 46.7 %collective-permute-start.18 = (bf16[64,4096]{1,0:T(8,128)(2,1)}, bf16[64,4096]{1,0:T(8,128)(2,1)S(1)}, u32[]{:S(2)}, u32[]{:S(2)}) collective-permute-start(bf16[64,4096]{1,0:T(8,128)(2,1)} %get-tuple-element.70), channel_id=1, source_target_pairs={{0,8},{4,12},{8,0},{12,4},{16,24},{20,28},{24,16},{28,20},{1,9},{5... | collective-permute-start | bytes 1572872 | tf_op jit(solution)/shard_map/ppermute | solution.py:16
  175.9 11.9 %collective-permute-start.15 = (bf16[64,4096]{1,0:T(8,128)(2,1)}, bf16[64,4096]{1,0:T(8,128)(2,1)}, u32[]{:S(2)}, u32[]{:S(2)}) collective-permute-start(bf16[64,4096]{1,0:T(8,128)(2,1)} %collective-permute-done.12), channel_id=1, source_target_pairs={{0,2},{1,3},{2,0},{3,1},{4,6},{5,7},{6,4},{7,5},{8,10},{9,11},{10,... | collective-permute-start | bytes 1572872 | tf_op jit(solution)/shard_map/ppermute | solution.py:16
  186.6 4.8 %copy-start.9 = (bf16[448,4096]{1,0:T(8,128)(2,1)S(1)}, bf16[448,4096]{1,0:T(8,128)(2,1)}, u32[]{:S(2)}) copy-start(bf16[448,4096]{1,0:T(8,128)(2,1)} %constant_dynamic-update-slice_fusion.2) | copy-start | bytes 11010052
  189.1 4.7 %copy-start.11 = (bf16[4096,512]{1,0:T(8,128)(2,1)S(1)}, bf16[4096,512]{1,0:T(8,128)(2,1)}, u32[]{:S(2)}) copy-start(bf16[4096,512]{1,0:T(8,128)(2,1)} %mul.62) | copy-start | bytes 12582916
  189.1 4.6 %collective-permute-start.16 = (bf16[128,4096]{1,0:T(8,128)(2,1)S(1)}, bf16[128,4096]{1,0:T(8,128)(2,1)S(1)}, u32[]{:S(2)}, u32[]{:S(2)}) collective-permute-start(bf16[128,4096]{1,0:T(8,128)(2,1)S(1)} %pad_maximum_fusion.1), channel_id=1, source_target_pairs={{0,1},{1,0},{2,3},{3,2},{4,5},{5,4},{6,7},{7,6},{8,9},{9,8},{10,11... | collective-permute-start | bytes 3145736 | tf_op jit(solution)/shard_map/ppermute | solution.py:16
  190.9 4.9 %collective-permute-start.14 = (bf16[224,4096]{1,0:T(8,128)(2,1)S(1)}, bf16[224,4096]{1,0:T(8,128)(2,1)S(1)}, u32[]{:S(2)}, u32[]{:S(2)}) collective-permute-start(bf16[224,4096]{1,0:T(8,128)(2,1)S(1)} %pad_maximum_fusion), channel_id=1, source_target_pairs={{0,1},{1,0},{2,3},{3,2},{4,5},{5,4},{6,7},{7,6},{8,9},{9,8},{10,11... | collective-permute-start | bytes 5505032 | tf_op jit(solution)/shard_map/ppermute | solution.py:16
  209.8 24.5 %collective-permute-start.19 = (bf16[64,4096]{1,0:T(8,128)(2,1)S(1)}, bf16[64,4096]{1,0:T(8,128)(2,1)S(1)}, u32[]{:S(2)}, u32[]{:S(2)}) collective-permute-start(bf16[64,4096]{1,0:T(8,128)(2,1)S(1)} %collective-permute-done.18), channel_id=1, source_target_pairs={{0,2},{1,3},{2,0},{3,1},{4,6},{5,7},{6,4},{7,5},{8,10},{9,11},{10,... | collective-permute-start | bytes 1572872 | tf_op jit(solution)/shard_map/ppermute | solution.py:16
  234.2 22.2 %copy-start.14 = (bf16[512,896]{1,0:T(8,128)(2,1)}, bf16[512,896]{1,0:T(8,128)(2,1)S(1)}, u32[]{:S(2)}) copy-start(bf16[512,896]{1,0:T(8,128)(2,1)S(1)} %collective-permute-done.21.refs_2_.refs_0_.refs_6_) | copy-start | bytes 2752516
  234.2 22.2 %collective-permute-start.22 = (bf16[512,896]{1,0:T(8,128)(2,1)S(1)}, bf16[512,896]{1,0:T(8,128)(2,1)S(1)}, u32[]{:S(2)}, u32[]{:S(2)}) collective-permute-start(bf16[512,896]{1,0:T(8,128)(2,1)S(1)} %collective-permute-done.21.refs_2_.refs_0_.refs_6_), channel_id=1, source_target_pairs={{0,4},{4,0},{8,12},{12,8},{16,20},{20,16},{24,28},{28,24},{1,5},{5... | collective-permute-start | bytes 2752520 | tf_op jit(solution)/shard_map/ppermute | solution.py:16
  235.5 51.8 %collective-permute-start.20 = (bf16[128,4096]{1,0:T(8,128)(2,1)}, bf16[128,4096]{1,0:T(8,128)(2,1)S(1)}, u32[]{:S(2)}, u32[]{:S(2)}) collective-permute-start(bf16[128,4096]{1,0:T(8,128)(2,1)} %pad_maximum_fusion.2), channel_id=1, source_target_pairs={{0,1},{1,0},{2,3},{3,2},{4,5},{5,4},{6,7},{7,6},{8,9},{9,8},{10,11... | collective-permute-start | bytes 3145736 | tf_op jit(solution)/shard_map/ppermute | solution.py:16
  280.2 7.2 %copy-start.12 = (bf16[4096,512]{1,0:T(8,128)(2,1)S(1)}, bf16[4096,512]{1,0:T(8,128)(2,1)}, u32[]{:S(2)}) copy-start(bf16[4096,512]{1,0:T(8,128)(2,1)} %mul.62) | copy-start | bytes 12582916
  297.9 8.5 %copy-start.26 = (f32[4,4096]{1,0:T(4,128)S(1)}, f32[4,4096]{1,0:T(4,128)}, u32[]{:S(2)}) copy-start(f32[4,4096]{1,0:T(4,128)} %get-tuple-element.90) | copy-start | bytes 196612
  297.9 8.5 %copy-start.27 = (f32[4,4096]{1,0:T(4,128)S(1)}, f32[4,4096]{1,0:T(4,128)}, u32[]{:S(2)}) copy-start(f32[4,4096]{1,0:T(4,128)} %get-tuple-element.91) | copy-start | bytes 196612
  298.0 8.5 %copy-start.28 = (f32[4,4096]{1,0:T(4,128)S(1)}, f32[4,4096]{1,0:T(4,128)}, u32[]{:S(2)}) copy-start(f32[4,4096]{1,0:T(4,128)} %get-tuple-element.92) | copy-start | bytes 196612
  298.0 8.5 %copy-start.29 = (f32[4,4096]{1,0:T(4,128)S(1)}, f32[4,4096]{1,0:T(4,128)}, u32[]{:S(2)}) copy-start(f32[4,4096]{1,0:T(4,128)} %get-tuple-element.94) | copy-start | bytes 196612
  298.0 8.5 %copy-start.30 = (f32[4,4096]{1,0:T(4,128)S(1)}, f32[4,4096]{1,0:T(4,128)}, u32[]{:S(2)}) copy-start(f32[4,4096]{1,0:T(4,128)} %get-tuple-element.95) | copy-start | bytes 196612
  298.0 8.5 %copy-start.31 = (f32[4,4096]{1,0:T(4,128)S(1)}, f32[4,4096]{1,0:T(4,128)}, u32[]{:S(2)}) copy-start(f32[4,4096]{1,0:T(4,128)} %get-tuple-element.96) | copy-start | bytes 196612
  298.0 8.5 %copy-start.32 = (f32[4,4096]{1,0:T(4,128)S(1)}, f32[4,4096]{1,0:T(4,128)}, u32[]{:S(2)}) copy-start(f32[4,4096]{1,0:T(4,128)} %get-tuple-element.93) | copy-start | bytes 196612
  298.0 10.0 %copy-start.21 = (f32[64,896]{1,0:T(8,128)S(1)}, f32[64,896]{1,0:T(8,128)}, u32[]{:S(2)}) copy-start(f32[64,896]{1,0:T(8,128)} %get-tuple-element.84) | copy-start | bytes 688132
  298.0 9.9 %copy-start.22 = (f32[64,896]{1,0:T(8,128)S(1)}, f32[64,896]{1,0:T(8,128)}, u32[]{:S(2)}) copy-start(f32[64,896]{1,0:T(8,128)} %get-tuple-element.85) | copy-start | bytes 688132
  298.0 9.9 %copy-start.23 = (f32[64,896]{1,0:T(8,128)S(1)}, f32[64,896]{1,0:T(8,128)}, u32[]{:S(2)}) copy-start(f32[64,896]{1,0:T(8,128)} %get-tuple-element.86) | copy-start | bytes 688132
  298.0 10.9 %copy-start.18 = (f32[64,896]{1,0:T(8,128)S(1)}, f32[64,896]{1,0:T(8,128)}, u32[]{:S(2)}) copy-start(f32[64,896]{1,0:T(8,128)} %get-tuple-element.60) | copy-start | bytes 688132
  298.0 10.9 %copy-start.19 = (f32[64,896]{1,0:T(8,128)S(1)}, f32[64,896]{1,0:T(8,128)}, u32[]{:S(2)}) copy-start(f32[64,896]{1,0:T(8,128)} %get-tuple-element.64) | copy-start | bytes 688132
  298.1 10.9 %copy-start.20 = (f32[64,896]{1,0:T(8,128)S(1)}, f32[64,896]{1,0:T(8,128)}, u32[]{:S(2)}) copy-start(f32[64,896]{1,0:T(8,128)} %get-tuple-element.69) | copy-start | bytes 688132
  298.1 10.9 %copy-start.24 = (f32[64,896]{1,0:T(8,128)S(1)}, f32[64,896]{1,0:T(8,128)}, u32[]{:S(2)}) copy-start(f32[64,896]{1,0:T(8,128)} %get-tuple-element.83) | copy-start | bytes 688132
  306.6 14.6 %copy-start.33 = (f32[1,896]{1,0:T(1,128)S(1)}, f32[1,896]{1,0:T(1,128)}, u32[]{:S(2)}) copy-start(f32[1,896]{1,0:T(1,128)} %get-tuple-element.61) | copy-start | bytes 10756
  306.6 14.6 %copy-start.34 = (f32[1,896]{1,0:T(1,128)S(1)}, f32[1,896]{1,0:T(1,128)}, u32[]{:S(2)}) copy-start(f32[1,896]{1,0:T(1,128)} %get-tuple-element.65) | copy-start | bytes 10756
  306.6 14.6 %copy-start.35 = (f32[1,896]{1,0:T(1,128)S(1)}, f32[1,896]{1,0:T(1,128)}, u32[]{:S(2)}) copy-start(f32[1,896]{1,0:T(1,128)} %get-tuple-element.72) | copy-start | bytes 10756
  306.6 14.6 %copy-start.36 = (f32[1,896]{1,0:T(1,128)S(1)}, f32[1,896]{1,0:T(1,128)}, u32[]{:S(2)}) copy-start(f32[1,896]{1,0:T(1,128)} %get-tuple-element.77) | copy-start | bytes 10756
  306.6 14.6 %copy-start.37 = (f32[1,896]{1,0:T(1,128)S(1)}, f32[1,896]{1,0:T(1,128)}, u32[]{:S(2)}) copy-start(f32[1,896]{1,0:T(1,128)} %get-tuple-element.79) | copy-start | bytes 10756
  306.6 14.6 %copy-start.38 = (f32[1,896]{1,0:T(1,128)S(1)}, f32[1,896]{1,0:T(1,128)}, u32[]{:S(2)}) copy-start(f32[1,896]{1,0:T(1,128)} %get-tuple-element.81) | copy-start | bytes 10756
  306.6 14.6 %copy-start.39 = (f32[1,896]{1,0:T(1,128)S(1)}, f32[1,896]{1,0:T(1,128)}, u32[]{:S(2)}) copy-start(f32[1,896]{1,0:T(1,128)} %get-tuple-element.87) | copy-start | bytes 10756
  306.6 14.6 %copy-start.40 = (f32[1,896]{1,0:T(1,128)S(1)}, f32[1,896]{1,0:T(1,128)}, u32[]{:S(2)}) copy-start(f32[1,896]{1,0:T(1,128)} %get-tuple-element.98) | copy-start | bytes 10756
  309.1 8.0 %collective-permute-start.23 = (f32[2,2,8,2304]{3,2,1,0:T(8,128)S(1)}, f32[2,2,8,2304]{3,2,1,0:T(8,128)S(1)}, u32[]{:S(2)}, u32[]{:S(2)}) collective-permute-start(f32[2,2,8,2304]{3,2,1,0:T(8,128)S(1)} %dynamic-slice_bitcast_fusion), channel_id=1, source_target_pairs={{0,4},{4,0},{8,12},{12,8},{16,20},{20,16},{24,28},{28,24},{1,5},{5... | collective-permute-start | bytes 884744 | tf_op jit(solution)/shard_map/ppermute | solution.py:16
  317.2 9.1 %collective-permute-start.24 = (f32[2,8,2304]{2,1,0:T(8,128)S(1)}, f32[2,8,2304]{2,1,0:T(8,128)S(1)}, u32[]{:S(2)}, u32[]{:S(2)}) collective-permute-start(f32[2,8,2304]{2,1,0:T(8,128)S(1)} %dynamic-slice_bitcast_fusion.1), channel_id=1, source_target_pairs={{0,16},{4,20},{8,24},{12,28},{16,0},{20,4},{24,8},{28,12},{1,17},{... | collective-permute-start | bytes 442376 | tf_op jit(solution)/shard_map/ppermute | solution.py:16
  329.6 10.8 %all-to-all-start.2 = ((f32[32,1,3]{2,1,0:T(1,128)}), f32[32,1,3]{2,1,0:T(1,128)S(1)}, u32[]{:S(2)}, u32[]{:S(2)}) async-start(f32[32,1,3]{2,1,0:T(1,128)} %broadcast_in_dim.8), calls=%async_computation.2 | async-start | bytes 32768 | tf_op jit(solution)/shard_map/all_to_all | solution.py:316
  334.4 17.2 %collective-permute-start.25 = (f32[8,1792]{1,0:T(8,128)S(1)}, f32[8,1792]{1,0:T(8,128)S(1)}, u32[]{:S(2)}, u32[]{:S(2)}) collective-permute-start(f32[8,1792]{1,0:T(8,128)S(1)} %dynamic-slice_bitcast_fusion.3), channel_id=1, source_target_pairs={{0,8},{4,12},{8,0},{12,4},{16,24},{20,28},{24,16},{28,20},{1,9},{5... | collective-permute-start | bytes 172040 | tf_op jit(solution)/shard_map/ppermute | solution.py:16
  340.4 8.0 %all-to-all-start.1 = ((f32[8,1,1024]{2,1,0:T(1,128)}), f32[8,1,1024]{2,1,0:T(1,128)S(1)}, u32[]{:S(2)}, u32[]{:S(2)}) async-start(f32[8,1,1024]{2,1,0:T(1,128)} %reshape.101), calls=%async_computation.1 | async-start | bytes 65536 | tf_op jit(solution)/shard_map/all_to_all | solution.py:331
  (6 other events, 7.6 us)
